TPU v7x, 256 devices: a whole 4x4x8 slice. The times are simulated.
256 devices in a mesh: ctx: 32 (over y, z), head: 8 (over x, core).
Axes of the slice: x: 4, y: 4, z: 8, core: 2. Of those that a mesh axis runs over, the one named last changes fastest.
Arguments:
- queries: bfloat16 [32768, 4096], P('ctx', 'head'), may hold values from -140 to 140
- keys: bfloat16 [32768, 1024], P('ctx', 'head'), may hold values from -8 to 8
- values: bfloat16 [32768, 1024], P('ctx', 'head'), may hold values from -6 to 6
- gates: int32 [32, 32, 3], P('ctx', 'head'), may hold values from 0 to 31, all different within a row; in each aligned block of 4 rows (0 to 3, 4 to 7, ..., all dimensions but the last counted through in order) at most 2 rows name the same one
- out_weight: bfloat16 [4096, 4096], P('head'), may hold values from -0.125 to 0.125
Outputs:
- attended: bfloat16 [32768, 4096], P('ctx', 'head')
Inputs may be any that keep to these rules, and one draw needn't show every extreme that they name: `gates`: the 3 entries of one query block and head are distinct. Within one query block and one group of 4 consecutive heads no key block is named more than 2 times, and some key block is named exactly 2 times. An entry that is not smaller than its query block's index selects nothing.
All inputs are finite; a program needn't handle non-finite values.
Results may differ from a plain program's by a relative error of at most 0.019.
Values may be sent and summed in bfloat16 or wider, within the bound.
A program may use at most 192 MiB of HBM per device.

v0:
```python
import jax
import jax.numpy as jnp
from jax import lax
from jax.sharding import PartitionSpec as P

QUERY_HEADS = 32
KEY_VALUE_HEADS = 8
HEAD_SIZE = 128


def attend_tile(q_tile, k_tile, v_tile, causal):
    scores = jnp.dot(q_tile, k_tile.T, preferred_element_type=jnp.float32) * q_tile.shape[-1] ** (
        -0.5
    )
    if causal:
        places = jnp.arange(q_tile.shape[0])
        scores = jnp.where(places[:, None] >= places[None, :], scores, -1e30)
    peak = jnp.max(scores, axis=1)
    expo = jnp.exp(scores - peak[:, None])
    total_row = jnp.sum(expo, axis=1)
    mixed = jnp.dot(expo.astype(jnp.bfloat16), v_tile, preferred_element_type=jnp.float32)
    return ((mixed / total_row[:, None]).astype(jnp.bfloat16), peak + jnp.log(total_row))


def merge_into(state, qblock, head_pos, out_tile, lse_row):
    peaks, totals, sums = state
    older = peaks[qblock, head_pos]
    newer = jnp.maximum(older, lse_row)
    keep_w = jnp.exp(older - newer)
    add_w = jnp.exp(lse_row - newer)
    return (
        peaks.at[qblock, head_pos].set(newer),
        totals.at[qblock, head_pos].set(totals[qblock, head_pos] * keep_w + add_w),
        sums.at[qblock, head_pos].set(
            sums[qblock, head_pos] * keep_w[:, None] + add_w[:, None] * out_tile.astype(jnp.float32)
        ),
    )


def shards(queries, keys, values, gates, out_weight):
    tok_rows = queries.shape[0]
    blocks_here = gates.shape[0]
    block_len = tok_rows // blocks_here
    head_size = HEAD_SIZE
    heads_here = queries.shape[1] // head_size
    kv_heads = keys.shape[1] // head_size
    query_group_size = QUERY_HEADS // KEY_VALUE_HEADS
    first_block = lax.axis_index("ctx") * blocks_here
    q_four = queries.reshape(blocks_here, block_len, heads_here, head_size)
    k_four = keys.reshape(blocks_here, block_len, kv_heads, head_size)
    v_four = values.reshape(blocks_here, block_len, kv_heads, head_size)
    qblock = 0
    row_out = []
    row_lse = []
    for head_pos in range(heads_here):
        kv_pos = head_pos // query_group_size
        tile_out, tile_lse = attend_tile(
            q_four[qblock, :, head_pos], k_four[qblock, :, kv_pos], v_four[qblock, :, kv_pos], True
        )
        row_out.append(tile_out.astype(jnp.float32))
        row_lse.append(tile_lse)
    own_out = [jnp.stack(row_out, 0)]
    own_lse = [jnp.stack(row_lse, 0)]
    peaks = jnp.stack(own_lse, 0)
    totals = jnp.ones_like(peaks)
    sums = jnp.stack(own_out, 0)
    state = (peaks, totals, sums)
    k_piece = lax.all_gather(keys, "ctx", axis=0, tiled=True)
    v_piece = lax.all_gather(values, "ctx", axis=0, tiled=True)
    piece_blocks = k_piece.shape[0] // block_len
    k_split = k_piece.reshape(piece_blocks, block_len, kv_heads, head_size)
    v_split = v_piece.reshape(piece_blocks, block_len, kv_heads, head_size)

    def visit(block_pos, state_now):
        k_tile_all = lax.dynamic_index_in_dim(k_split, block_pos, 0, False)
        v_tile_all = lax.dynamic_index_in_dim(v_split, block_pos, 0, False)
        qblock = 0
        for head_pos in range(heads_here):
            kv_pos = head_pos // query_group_size
            picked = jnp.any(gates[qblock, head_pos] == block_pos) & (
                block_pos < first_block + qblock
            )

            def update(state_arg, qblock=qblock, head_pos=head_pos, kv_pos=kv_pos):
                tile_out, tile_lse = attend_tile(
                    q_four[qblock, :, head_pos], k_tile_all[:, kv_pos], v_tile_all[:, kv_pos], False
                )
                return merge_into(state_arg, qblock, head_pos, tile_out, tile_lse)

            def unchanged(state_arg):
                return state_arg

            state_now = lax.cond(picked, update, unchanged, state_now)
        return state_now

    state = lax.fori_loop(0, piece_blocks, visit, state)
    peaks, totals, sums = state
    attention = (sums / totals[..., None]).astype(jnp.bfloat16)
    attention = jnp.transpose(attention, (0, 2, 1, 3)).reshape(tok_rows, heads_here * head_size)
    term = jnp.dot(attention, out_weight, preferred_element_type=jnp.float32)
    return lax.psum_scatter(term.astype(jnp.bfloat16), "head", scatter_dimension=1, tiled=True)


def solution(mesh):
    return jax.shard_map(
        shards,
        mesh=mesh,
        in_specs=(
            P("ctx", "head"),
            P("ctx", "head"),
            P("ctx", "head"),
            P("ctx", "head", None),
            P("head", None),
        ),
        out_specs=P("ctx", "head"),
        check_vma=False,
    )
```

profile of v0, /device:TPU:233, one launch (start us, length us, event | category | flops | bytes accessed | tf_op | source)
XLA Modules:
  0.0 570.0 jit_solution(5924775418221649727)
XLA Ops:
  18.7 86.5 %all-gather.3.cloned.1.call-done = bf16[32768,128]{1,0:T(8,128)(2,1)} async-done(((bf16[1024,128]{1,0:T(8,128)(2,1)}), bf16[32768,128]{1,0:T(8,128)(2,1)}) %all-gather.3.cloned.1.call-update) | async-done | bytes 8388624 | tf_op jit(solution)/shard_map/all_gather | solution.py:68
  105.2 98.2 %all-gather.5.cloned.1.call-done = bf16[32768,128]{1,0:T(8,128)(2,1)} async-done(((bf16[1024,128]{1,0:T(8,128)(2,1)}), bf16[32768,128]{1,0:T(8,128)(2,1)}) %all-gather.5.cloned.1.call-update) | async-done | bytes 8388624 | tf_op jit(solution)/shard_map/all_gather | solution.py:69
  203.4 263.1 %while.29 = (s32[]{:T(128)}, f32[1,4,1024]{2,1,0:T(4,128)S(1)}, f32[1,4,1024]{2,1,0:T(4,128)S(1)}, f32[1,4,1024,128]{3,2,1,0:T(8,128)S(1)}, s32[1,4,3]{1,0,2:T(1...) while((s32[]{:T(128)}, f32[1,4,1024]{2,1,0:T(4,128)S(1)}, ...), condition=%wide.region_33.34_spmd, body=%wide.region_8.33_spmd.sunk | while | flops 2184482816 | bytes 132564040 | solution.py:96
  213.7 13.1 %conditional.11 = ((f32[1,4,1024]{2,1,0:T(4,128)S(1)}, f32[1,4,1024]{2,1,0:T(4,128)S(1)}, f32[1,4,1024,128]{3,2,1,0:T(8,128)S(1)})) conditional(s32[]{:T(128)} %convert_element_type.314, (f32[1,4,1024]{2,1,0:T(4,128)S(1)}, f32[1,4,1024]{2,1,0:T(4,128)S(1)}, f32[1,4,1024,128]{3,2,1,0:T(8,128)S(1)}) %get-tuple-element.632, ...), branch_computations={%region_27.27_spmd, %region_28.32_spmd} | conditional | flops 546187264 | bytes 33931532 | solution.py:93
  222.5 4.3 fusion.135
  237.1 13.6 %conditional.10 = ((f32[1,4,1024]{2,1,0:T(4,128)S(1)}, f32[1,4,1024]{2,1,0:T(4,128)S(1)}, f32[1,4,1024,128]{3,2,1,0:T(8,128)S(1)})) conditional(s32[]{:T(128)} %convert_element_type.315, (f32[1,4,1024]{2,1,0:T(4,128)S(1)}, f32[1,4,1024]{2,1,0:T(4,128)S(1)}, f32[1,4,1024,128]{3,2,1,0:T(8,128)S(1)}) %get-tuple-element.631, ...), branch_computations={%region_21.21_spmd, %region_22.26_spmd} | conditional | flops 546187264 | bytes 32882928 | solution.py:93
  246.3 4.4 fusion.97
  261.0 9.4 %conditional.9 = ((f32[1,4,1024]{2,1,0:T(4,128)S(1)}, f32[1,4,1024]{2,1,0:T(4,128)S(1)}, f32[1,4,1024,128]{3,2,1,0:T(8,128)S(1)})) conditional(s32[]{:T(128)} %convert_element_type.316, (f32[1,4,1024]{2,1,0:T(4,128)S(1)}, f32[1,4,1024]{2,1,0:T(4,128)S(1)}, f32[1,4,1024,128]{3,2,1,0:T(8,128)S(1)}) %get-tuple-element.630, ...), branch_computations={%region_17.17_spmd, %region_18.0_spmd} | conditional | flops 546054144 | bytes 32350296 | solution.py:93
  261.7 1.9 copy-done.2
  266.7 3.7 fusion.59
  275.6 6.7 %conditional.8 = ((f32[1,4,1024]{2,1,0:T(4,128)S(1)}, f32[1,4,1024]{2,1,0:T(4,128)S(1)}, f32[1,4,1024,128]{3,2,1,0:T(8,128)S(1)})) conditional(s32[]{:T(128)} %convert_element_type.317, (f32[1,4,1024]{2,1,0:T(4,128)S(1)}, f32[1,4,1024]{2,1,0:T(4,128)S(1)}, f32[1,4,1024,128]{3,2,1,0:T(8,128)S(1)}) %tuple.131, (f32[1,4,1024]{2,1,0:T(4,128)S(1)}, ...), branch_computations={%region_13.13_spmd, %region_14.16_spmd} | conditional | flops 546054144 | bytes 32350276 | solution.py:93
  279.2 3.0 fusion.24
  287.5 13.1 %conditional.11 = ((f32[1,4,1024]{2,1,0:T(4,128)S(1)}, f32[1,4,1024]{2,1,0:T(4,128)S(1)}, f32[1,4,1024,128]{3,2,1,0:T(8,128)S(1)})) conditional(s32[]{:T(128)} %convert_element_type.314, (f32[1,4,1024]{2,1,0:T(4,128)S(1)}, f32[1,4,1024]{2,1,0:T(4,128)S(1)}, f32[1,4,1024,128]{3,2,1,0:T(8,128)S(1)}) %get-tuple-element.632, ...), branch_computations={%region_27.27_spmd, %region_28.32_spmd} | conditional | flops 546187264 | bytes 33931532 | solution.py:93
  296.3 4.3 fusion.135
  305.7 13.6 %conditional.10 = ((f32[1,4,1024]{2,1,0:T(4,128)S(1)}, f32[1,4,1024]{2,1,0:T(4,128)S(1)}, f32[1,4,1024,128]{3,2,1,0:T(8,128)S(1)})) conditional(s32[]{:T(128)} %convert_element_type.315, (f32[1,4,1024]{2,1,0:T(4,128)S(1)}, f32[1,4,1024]{2,1,0:T(4,128)S(1)}, f32[1,4,1024,128]{3,2,1,0:T(8,128)S(1)}) %get-tuple-element.631, ...), branch_computations={%region_21.21_spmd, %region_22.26_spmd} | conditional | flops 546187264 | bytes 32882928 | solution.py:93
  315.0 4.4 fusion.97
  334.8 9.4 %conditional.9 = ((f32[1,4,1024]{2,1,0:T(4,128)S(1)}, f32[1,4,1024]{2,1,0:T(4,128)S(1)}, f32[1,4,1024,128]{3,2,1,0:T(8,128)S(1)})) conditional(s32[]{:T(128)} %convert_element_type.316, (f32[1,4,1024]{2,1,0:T(4,128)S(1)}, f32[1,4,1024]{2,1,0:T(4,128)S(1)}, f32[1,4,1024,128]{3,2,1,0:T(8,128)S(1)}) %get-tuple-element.630, ...), branch_computations={%region_17.17_spmd, %region_18.0_spmd} | conditional | flops 546054144 | bytes 32350296 | solution.py:93
  340.4 3.7 fusion.59
  359.6 6.7 %conditional.8 = ((f32[1,4,1024]{2,1,0:T(4,128)S(1)}, f32[1,4,1024]{2,1,0:T(4,128)S(1)}, f32[1,4,1024,128]{3,2,1,0:T(8,128)S(1)})) conditional(s32[]{:T(128)} %convert_element_type.317, (f32[1,4,1024]{2,1,0:T(4,128)S(1)}, f32[1,4,1024]{2,1,0:T(4,128)S(1)}, f32[1,4,1024,128]{3,2,1,0:T(8,128)S(1)}) %tuple.131, (f32[1,4,1024]{2,1,0:T(4,128)S(1)}, ...), branch_computations={%region_13.13_spmd, %region_14.16_spmd} | conditional | flops 546054144 | bytes 32350276 | solution.py:93
  363.2 3.0 fusion.24
  366.3 13.1 %conditional.11 = ((f32[1,4,1024]{2,1,0:T(4,128)S(1)}, f32[1,4,1024]{2,1,0:T(4,128)S(1)}, f32[1,4,1024,128]{3,2,1,0:T(8,128)S(1)})) conditional(s32[]{:T(128)} %convert_element_type.314, (f32[1,4,1024]{2,1,0:T(4,128)S(1)}, f32[1,4,1024]{2,1,0:T(4,128)S(1)}, f32[1,4,1024,128]{3,2,1,0:T(8,128)S(1)}) %get-tuple-element.632, ...), branch_computations={%region_27.27_spmd, %region_28.32_spmd} | conditional | flops 546187264 | bytes 33931532 | solution.py:93
  375.2 4.3 fusion.135
  470.3 9.0 %convolution_convert_fusion = bf16[1024,4096]{1,0:T(8,128)(2,1)} fusion(bf16[1024,512]{0,1:T(8,128)(2,1)S(1)} %bitcast.171, bf16[512,4096]{1,0:T(8,128)(2,1)} %param.43), kind=kOutput, calls=%fused_computation.126 | convolution fusion | flops 4299161600 | bytes 13631488 | tf_op jit(solution)/shard_map/dot_general | solution.py:100
  479.2 84.2 %reduce-scatter.2.cloned.1.call-done = bf16[1024,512]{1,0:T(8,128)(2,1)} async-done(((bf16[1024,4096]{1,0:T(8,128)(2,1)}), bf16[1024,512]{1,0:T(8,128)(2,1)}) %reduce-scatter.2.cloned.1.call-update) | async-done | bytes 1048592 | tf_op jit(solution)/shard_map/reduce_scatter | solution.py:101
  (356 shorter events, 160.2 us)
Async XLA Ops:
  6.5 3.7 copy-start.6
  6.5 98.7 %all-gather.3.cloned.1.call-start = ((), (), s32[]{:S(2)}) async-start(), calls=%async_computation.1 | async-start | bytes 8650752 | tf_op jit(solution)/shard_map/all_gather | solution.py:68
  7.3 196.2 %all-gather.5.cloned.1.call-start = ((), (), s32[]{:S(2)}) async-start(), calls=%async_computation.2 | async-start | bytes 8650752 | tf_op jit(solution)/shard_map/all_gather | solution.py:69
  8.0 555.4 %reduce-scatter.2.cloned.1.call-start = ((), (), s32[]{:S(2)}) async-start(), calls=%async_computation.3 | async-start | bytes 9437184 | tf_op jit(solution)/shard_map/reduce_scatter | solution.py:101
  14.0 1.3 copy-start.7
  17.7 185.7 %copy-start.5 = (s32[1,4,3]{1,0,2:T(1,128)S(1)}, s32[1,4,3]{1,0,2:T(1,128)}, u32[]{:S(2)}) copy-start(s32[1,4,3]{1,0,2:T(1,128)} %param.42) | copy-start | bytes 148
  215.7 6.0 %copy-start.9 = (s32[4]{0:T(128)S(1)}, s32[4]{0:T(128)}, u32[]{:S(2)}) copy-start(s32[4]{0:T(128)} %constant.355.clone) | copy-start | bytes 52 | tf_op jit(solution)/shard_map/while/body/eval_jaxpr/cond
  216.4 1.9 copy-start.1
  216.4 6.1 %copy-start.4 = (bf16[1024,1,128]{2,0,1:T(8,128)(2,1)S(1)}, bf16[1024,1,128]{2,0,1:T(8,128)(2,1)}, u32[]{:S(2)}) copy-start(bf16[1024,1,128]{2,0,1:T(8,128)(2,1)} %get-tuple-element.393) | copy-start | bytes 786436 | tf_op jit(solution)/shard_map/while/body/eval_jaxpr/cond
  239.2 6.4 %copy-start.8 = (s32[4]{0:T(128)S(1)}, s32[4]{0:T(128)}, u32[]{:S(2)}) copy-start(s32[4]{0:T(128)} %constant.346.clone) | copy-start | bytes 52 | tf_op jit(solution)/shard_map/while/body/eval_jaxpr/cond
  239.9 1.9 copy-start
  261.7 1.9 copy-start.2
  276.3 1.9 copy-start.3
  289.5 6.0 %copy-start.9 = (s32[4]{0:T(128)S(1)}, s32[4]{0:T(128)}, u32[]{:S(2)}) copy-start(s32[4]{0:T(128)} %constant.355.clone) | copy-start | bytes 52 | tf_op jit(solution)/shard_map/while/body/eval_jaxpr/cond
  290.2 1.9 copy-start.1
  290.2 6.1 %copy-start.4 = (bf16[1024,1,128]{2,0,1:T(8,128)(2,1)S(1)}, bf16[1024,1,128]{2,0,1:T(8,128)(2,1)}, u32[]{:S(2)}) copy-start(bf16[1024,1,128]{2,0,1:T(8,128)(2,1)} %get-tuple-element.393) | copy-start | bytes 786436 | tf_op jit(solution)/shard_map/while/body/eval_jaxpr/cond
  307.8 6.3 %copy-start.8 = (s32[4]{0:T(128)S(1)}, s32[4]{0:T(128)}, u32[]{:S(2)}) copy-start(s32[4]{0:T(128)} %constant.346.clone) | copy-start | bytes 52 | tf_op jit(solution)/shard_map/while/body/eval_jaxpr/cond
  308.5 1.9 copy-start
  335.5 1.9 copy-start.2
  360.3 1.9 copy-start.3
  368.4 6.0 %copy-start.9 = (s32[4]{0:T(128)S(1)}, s32[4]{0:T(128)}, u32[]{:S(2)}) copy-start(s32[4]{0:T(128)} %constant.355.clone) | copy-start | bytes 52 | tf_op jit(solution)/shard_map/while/body/eval_jaxpr/cond
  369.1 1.9 copy-start.1
  369.1 6.1 %copy-start.4 = (bf16[1024,1,128]{2,0,1:T(8,128)(2,1)S(1)}, bf16[1024,1,128]{2,0,1:T(8,128)(2,1)}, u32[]{:S(2)}) copy-start(bf16[1024,1,128]{2,0,1:T(8,128)(2,1)} %get-tuple-element.393) | copy-start | bytes 786436 | tf_op jit(solution)/shard_map/while/body/eval_jaxpr/cond
Sparse Core Ops, SparseCore 0:
  10.0 95.2 all-gather.2
  107.8 95.5 all-gather.4
  479.4 84.0 reduce-scatter.1
where the time goes:
time: 576 us; the launch traced here: 570 us
  waiting for transfers between devices  270 us (47%)
  local copies, waits for them, and re-layouts  92.7 us (16%)
  loops' own time  81.9 us (14%)
  matrix products  56.5 us (10%)
  other arithmetic  55.2 us (10%)
  between operations  13.2 us (2%)
    all_gather x1, waiting for transfers between devices, shards(): v_piece = lax.all_gather(values, 'ctx', axis=0, tiled=True)  98.2 us
    all_gather x1, waiting for transfers between devices, shards(): k_piece = lax.all_gather(keys, 'ctx', axis=0, tiled=True)  86.5 us
    reduce_scatter x1, waiting for transfers between devices, shards(): lax.psum_scatter(term.astype(jnp.bfloat16), 'head', scatter_dimension=1,...  84.2 us
    another operation x1, loops' own time, shards(): state = lax.fori_loop(0, piece_blocks, visit, state)  81 us
    squeeze x32, local copies, waits for them, and re-layouts, visit(): v_tile_all = lax.dynamic_index_in_dim(v_split, block_pos, 0, False)  56.7 us
    dot_general x13, matrix products, attend_tile(): jnp.dot(expo.astype(jnp.bfloat16), v_tile, preferred_element_type=jnp.flo...  38.3 us
    reduce_or x32, other arithmetic, visit(): jnp.any(gates[qblock, head_pos] == block_pos)  26.4 us
    another operation x20, other arithmetic  17.7 us
  transfers between devices with their start and end apart: 3, of which 3 were waited for; matrix products, arithmetic and copies ran while one was open for 2% of the time, Pallas kernels for 0%

commit v1 on v0

v1 whole, which is shorter than its diff:
```python
import functools

import jax
import jax.numpy as jnp
from jax import lax
from jax.experimental import pallas as pl
from jax.experimental.pallas import tpu as pltpu
from jax.sharding import PartitionSpec as P

MESH = pl.DeviceIdType.MESH
F32 = jnp.float32
BF16 = jnp.bfloat16
TOK = 1024
HS = 128
HQ = 4
TOPK = 3
NY = 4
NZ = 8
NX = 4
SCALE2 = HS**-0.5 * 1.4426950408889634
LOW = -1e30
VMEM_LIMIT = 56 * 1024 * 1024
QCH = 4


def dev(ctx, head):
    return (ctx, head)


def gather_kernel(q_ref, k_ref, v_ref, g_ref, qa, ka, va, ga, kv_s, kv_r, q_s, q_r, g_s, g_r, loc):
    ctx = lax.axis_index("ctx")
    head = lax.axis_index("head")
    y = ctx // NZ
    z = ctx % NZ
    up = y * NZ + (z + 1) % NZ
    down = y * NZ + (z + NZ - 1) % NZ
    column = [((y + d) % NY) * NZ + z for d in (1, 2, 3)]

    barrier = pltpu.get_barrier_semaphore()
    for other in [up, down] + column:
        pl.semaphore_signal(barrier, inc=1, device_id=dev(other, head), device_id_type=MESH)
    pl.semaphore_wait(barrier, 5)

    def remote(src, dst, s, r, to):
        return pltpu.make_async_remote_copy(
            src_ref=src, dst_ref=dst, send_sem=s, recv_sem=r, device_id=dev(to, head), device_id_type=MESH
        )

    def ring_copy(direction, step, part):
        block = (z + NZ - step) % NZ if direction == 0 else (z + step) % NZ
        own, out = (k_ref, ka) if part == 0 else (v_ref, va)
        src = own if step == 0 else out.at[block]
        return remote(
            src, out.at[block], kv_s.at[direction, step, part], kv_r.at[direction, step, part], up if direction == 0 else down
        )

    def parts(direction, step):
        return (0, 1) if step < 3 else (direction,)

    own_copies = [
        pltpu.make_async_copy(k_ref, ka.at[z], loc.at[0]),
        pltpu.make_async_copy(v_ref, va.at[z], loc.at[1]),
        pltpu.make_async_copy(q_ref, qa.at[0], loc.at[2]),
        pltpu.make_async_copy(g_ref, ga.at[0], loc.at[3]),
    ]
    rows = TOK // QCH

    def q_copy(kind, c):
        at = pl.ds(c * rows, rows)
        if kind == 0:
            return remote(q_ref.at[at], qa.at[1, at], q_s.at[0, c], q_r.at[0, c], column[2])
        if kind == 1:
            return remote(qa.at[1, at], qa.at[2, at], q_s.at[1, c], q_r.at[1, c], column[2])
        return remote(q_ref.at[at], qa.at[3, at], q_s.at[2, c], q_r.at[2, c], column[0])

    for part in (0, 1):
        for direction in (0, 1):
            ring_copy(direction, 0, part).start()

    @pl.when(y >= 1)
    def _():
        for c in range(QCH):
            q_copy(0, c).start()

    @pl.when(y == NY - 1)
    def _():
        for c in range(QCH):
            q_copy(2, c).start()

    g_copies = [remote(g_ref, ga.at[NY - d], g_s.at[d - 1], g_r.at[d - 1], column[d - 1]) for d in (1, 2, 3)]
    for c in g_copies:
        c.start()
    for c in own_copies:
        c.start()

    for step in range(4):
        for part in (0, 1):
            for direction in (0, 1):
                if part in parts(direction, step):
                    ring_copy(direction, step, part).wait_recv()
                    if step < 3 and part in parts(direction, step + 1):
                        ring_copy(direction, step + 1, part).start()
        if step < 3:

            @pl.when((y >= 1) & (y + 1 < NY))
            def _(step=step):
                for c in (step,) if step < 2 else (2, 3):
                    q_copy(0, c).wait_recv()
                    q_copy(1, c).start()

    @pl.when(y == 0)
    def _():
        for c in range(QCH):
            q_copy(0, c).wait_recv()
            q_copy(2, c).wait_recv()

    @pl.when(y + 2 < NY)
    def _():
        for c in range(QCH):
            q_copy(1, c).wait_recv()

    @pl.when(y >= 1)
    def _():
        for c in range(QCH):
            q_copy(0, c).wait_send()

    @pl.when((y >= 1) & (y + 1 < NY))
    def _():
        for c in range(QCH):
            q_copy(1, c).wait_send()

    @pl.when(y == NY - 1)
    def _():
        for c in range(QCH):
            q_copy(2, c).wait_send()

    for step in range(4):
        for direction in (0, 1):
            for part in parts(direction, step):
                ring_copy(direction, step, part).wait_send()
    for c in g_copies:
        c.wait()
    for c in own_copies:
        c.wait()


def gather(q, k, v, g):
    hbm = pl.BlockSpec(memory_space=pl.ANY)
    return pl.pallas_call(
        gather_kernel,
        out_shape=(
            jax.ShapeDtypeStruct((NY, TOK, HQ * HS), BF16),
            jax.ShapeDtypeStruct((NZ, TOK, HS), BF16),
            jax.ShapeDtypeStruct((NZ, TOK, HS), BF16),
            jax.ShapeDtypeStruct((NY, 8, 128), jnp.int32),
        ),
        in_specs=[hbm] * 4,
        out_specs=(hbm,) * 4,
        scratch_shapes=[
            pltpu.SemaphoreType.DMA((2, 4, 2)),
            pltpu.SemaphoreType.DMA((2, 4, 2)),
            pltpu.SemaphoreType.DMA((3, QCH)),
            pltpu.SemaphoreType.DMA((3, QCH)),
            pltpu.SemaphoreType.DMA((3,)),
            pltpu.SemaphoreType.DMA((3,)),
            pltpu.SemaphoreType.DMA((4,)),
        ],
        compiler_params=pltpu.CompilerParams(
            collective_id=0, has_side_effects=True, vmem_limit_bytes=VMEM_LIMIT
        ),
        name="gather",
    )(q, k, v, g)


RT = 256


def attend_kernel(gates, place, q_ref, k_ref, v_ref, out_ref, lse_ref, peak, acc, todo):
    slot = pl.program_id(0)
    head = pl.program_id(1)
    y = place[0]
    z = place[1]
    mine = (y + slot) * NZ + z

    def tile(i, k_tile, v_ext, first, diagonal):
        at = pl.ds(i * RT, RT)
        s = lax.dot_general(
            q_ref[0, at, :], k_tile, (((1,), (1,)), ((), ())), preferred_element_type=F32
        )
        if diagonal:
            keys = k_tile.shape[0]
            r = lax.broadcasted_iota(jnp.int32, (RT, keys), 0) + (keys - RT)
            c = lax.broadcasted_iota(jnp.int32, (RT, keys), 1)
            s = jnp.where(r >= c, s, LOW)
        top = jnp.max(s, axis=1, keepdims=True) * SCALE2
        if first:
            new = jnp.broadcast_to(top, (RT, HS))
        else:
            old = peak[at, :]
            new = jnp.maximum(old, top)
        p = jnp.exp2(s * SCALE2 - new[:, :1]).astype(BF16)
        part = jnp.dot(p, v_ext, preferred_element_type=F32)
        if first:
            acc[at, :] = part
        else:
            fade = jnp.exp2(old - new)
            acc[at, :] = acc[at, :] * jnp.concatenate([fade, fade], axis=1) + part
        peak[at, :] = new

    def extended(block, n):
        v = v_ref[block, 0:n, :]
        return jnp.concatenate([v, jnp.ones_like(v)], axis=1)

    count = jnp.int32(0)
    for j in range(TOPK):
        g = gates[slot * (HQ * TOPK) + head * TOPK + j]
        good = (g >= y * NZ) & (g < (y + 1) * NZ) & (g < mine) & (y + slot < NY)

        @pl.when(good)
        def _(g=g, count=count):
            todo[count] = g - y * NZ

        count = count + good.astype(jnp.int32)

    @pl.when(slot == 0)
    def _():
        for i in range(TOK // RT):
            n = (i + 1) * RT
            tile(i, k_ref[z, 0:n, :], extended(z, n), True, True)

    @pl.when((slot > 0) & (count > 0))
    def _():
        block = todo[0]
        for i in range(TOK // RT):
            tile(i, k_ref[block], extended(block, TOK), True, False)

    def more(e, carry):
        block = todo[e]
        for i in range(TOK // RT):
            tile(i, k_ref[block], extended(block, TOK), False, False)
        return carry

    lax.fori_loop(jnp.where(slot == 0, 0, 1), count, more, 0)

    some = (slot == 0) | (count > 0)

    @pl.when(some)
    def _():
        for i in range(TOK // RT):
            at = pl.ds(i * RT, RT)
            total = acc[at, HS:]
            out_ref[0, at, :] = (acc[at, :HS] / total).astype(BF16)
            lse = peak[at, :] + jnp.log2(total)
            lse_ref[0, pl.ds(head, 1), at] = lse.T[0:1, :]

    @pl.when(jnp.logical_not(some))
    def _():
        out_ref[...] = jnp.zeros_like(out_ref)
        lse_ref[0, pl.ds(head, 1), :] = jnp.full((1, TOK), LOW, F32)


def attend(gates, place, qa, ka, va):
    return pl.pallas_call(
        attend_kernel,
        out_shape=(
            jax.ShapeDtypeStruct((NY, TOK, HQ * HS), BF16),
            jax.ShapeDtypeStruct((NY, 8, TOK), F32),
        ),
        grid_spec=pltpu.PrefetchScalarGridSpec(
            num_scalar_prefetch=2,
            grid=(NY, HQ),
            in_specs=[
                pl.BlockSpec((1, TOK, HS), lambda s, h, *_: (s, 0, h)),
                pl.BlockSpec((NZ, TOK, HS), lambda s, h, *_: (0, 0, 0)),
                pl.BlockSpec((NZ, TOK, HS), lambda s, h, *_: (0, 0, 0)),
            ],
            out_specs=(
                pl.BlockSpec((1, TOK, HS), lambda s, h, *_: (s, 0, h)),
                pl.BlockSpec((1, 8, TOK), lambda s, h, *_: (s, 0, 0)),
            ),
            scratch_shapes=[
                pltpu.VMEM((TOK, HS), F32),
                pltpu.VMEM((TOK, 2 * HS), F32),
                pltpu.SMEM((TOPK + 1,), jnp.int32),
            ],
        ),
        compiler_params=pltpu.CompilerParams(vmem_limit_bytes=VMEM_LIMIT),
        name="attend",
    )(gates, place, qa, ka, va)


NC = 8
CR = TOK // NC
HF = CR // 2


def project_kernel(a_ref, w_ref, out_ref, sib_out, sib_in, own, a_out, a_in, b_out, b_in, ss, sr, as_, ar, bs, br):
    ctx = lax.axis_index("ctx")
    head = lax.axis_index("head")
    x = head // 2
    core = head % 2
    sibling = x * 2 + (1 - core)
    right = ((x + 1) % NX) * 2 + core
    left = ((x + NX - 1) % NX) * 2 + core
    beside = [right, left]
    width = HQ * HS

    barrier = pltpu.get_barrier_semaphore()
    for other in [sibling, right, left]:
        pl.semaphore_signal(barrier, inc=1, device_id=dev(ctx, other), device_id_type=MESH)
    pl.semaphore_wait(barrier, 3)

    def remote(src, dst, s, r, to):
        return pltpu.make_async_remote_copy(
            src_ref=src, dst_ref=dst, send_sem=s, recv_sem=r, device_id=dev(ctx, to), device_id_type=MESH
        )

    def sib_copy(r):
        return remote(sib_out.at[r], sib_in.at[r], ss.at[r], sr.at[r], sibling)

    def a_copy(r, side):
        return remote(a_out.at[r, side], a_in.at[r, side], as_.at[r, side], ar.at[r, side], beside[side])

    def b_copy(r, side):
        return remote(b_out.at[r, side], b_in.at[r, side], bs.at[r, side], br.at[r, side], beside[side])

    def columns(k, c):
        return pl.ds(pl.multiple_of((((x + k) % NX) * 2 + c) * width, width), width)

    def stage0(r):
        rows = a_ref[pl.ds(pl.multiple_of(r * CR, CR), CR), :]
        for k in range(NX):
            t = jnp.dot(rows, w_ref[:, columns(k, 1 - core)], preferred_element_type=F32)
            sib_out[r, k] = t.astype(BF16)
        sib_copy(r).start()
        for k in range(NX):
            own[r, k] = jnp.dot(rows, w_ref[:, columns(k, core)], preferred_element_type=F32).astype(BF16)

    def pair(r, k, at):
        return own[r, k, at, :].astype(F32) + sib_in[r, k, at, :].astype(F32)

    def stage1(r):
        sib_copy(r).wait_recv()
        for side in (0, 1):
            a_out[r, side] = pair(r, 2, pl.ds(side * HF, HF)).astype(BF16)
            a_copy(r, side).start()

    def stage2(r):
        for side in (0, 1):
            k = 1 if side == 0 else 3
            a_copy(r, side).wait_recv()
            with_a = pl.ds(side * HF, HF)
            without = pl.ds((1 - side) * HF, HF)
            b_out[r, side, with_a, :] = (pair(r, k, with_a) + a_in[r, side].astype(F32)).astype(BF16)
            b_out[r, side, without, :] = pair(r, k, without).astype(BF16)
            b_copy(r, side).start()

    def stage3(r):
        b_copy(r, 0).wait_recv()
        b_copy(r, 1).wait_recv()
        total = pair(r, 0, pl.ds(0, CR)) + b_in[r, 0].astype(F32) + b_in[r, 1].astype(F32)
        out_ref[pl.ds(pl.multiple_of(r * CR, CR), CR), :] = total.astype(BF16)

    def step(t, carry):
        @pl.when(t < NC)
        def _():
            stage0(t)

        @pl.when((t >= 1) & (t < NC + 1))
        def _():
            stage1(t - 1)

        @pl.when((t >= 2) & (t < NC + 2))
        def _():
            stage2(t - 2)

        @pl.when(t >= 3)
        def _():
            stage3(t - 3)

        return carry

    lax.fori_loop(0, NC + 3, step, 0)

    def finish(r, carry):
        sib_copy(r).wait_send()
        for side in (0, 1):
            a_copy(r, side).wait_send()
            b_copy(r, side).wait_send()
        return carry

    lax.fori_loop(0, NC, finish, 0)


def project(attention, weight):
    width = HQ * HS
    vmem = pl.BlockSpec(memory_space=pltpu.VMEM)
    return pl.pallas_call(
        project_kernel,
        out_shape=jax.ShapeDtypeStruct((TOK, width), BF16),
        in_specs=[vmem] * 2,
        out_specs=vmem,
        scratch_shapes=[
            pltpu.VMEM((NC, NX, CR, width), BF16),
            pltpu.VMEM((NC, NX, CR, width), BF16),
            pltpu.VMEM((NC, NX, CR, width), BF16),
            pltpu.VMEM((NC, 2, HF, width), BF16),
            pltpu.VMEM((NC, 2, HF, width), BF16),
            pltpu.VMEM((NC, 2, CR, width), BF16),
            pltpu.VMEM((NC, 2, CR, width), BF16),
            pltpu.SemaphoreType.DMA((NC,)),
            pltpu.SemaphoreType.DMA((NC,)),
            pltpu.SemaphoreType.DMA((NC, 2)),
            pltpu.SemaphoreType.DMA((NC, 2)),
            pltpu.SemaphoreType.DMA((NC, 2)),
            pltpu.SemaphoreType.DMA((NC, 2)),
        ],
        compiler_params=pltpu.CompilerParams(
            collective_id=1, has_side_effects=True, vmem_limit_bytes=VMEM_LIMIT
        ),
        name="project",
    )(attention, weight)


def merge(partial, lse):
    y = lax.axis_index("ctx") // NZ
    outs = [partial[0]]
    lses = [lse[0, :HQ]]
    for d in (1, 2, 3):
        pairs = [((yy * NZ + zz), ((yy + d) % NY) * NZ + zz) for yy in range(NY) for zz in range(NZ)]
        got = lax.ppermute(partial[d], "ctx", pairs)
        got_lse = lax.ppermute(lse[d], "ctx", pairs)
        outs.append(got)
        lses.append(jnp.where(y >= d, got_lse[:HQ], LOW))
    lses = jnp.stack(lses, 0)
    top = jnp.max(lses, axis=0)
    w = jnp.exp2(lses - top[None])
    w = w / jnp.sum(w, axis=0)[None]
    total = 0.0
    for d in range(NY):
        wide = jnp.repeat(w[d].T, HS, axis=1)
        total = total + wide * outs[d].astype(F32)
    return total.astype(BF16)


def shards(queries, keys, values, gates, out_weight):
    ctx = lax.axis_index("ctx")
    padded = jnp.zeros((8, 128), jnp.int32).at[0, : HQ * TOPK].set(gates.reshape(-1))
    qa, ka, va, ga = gather(queries, keys, values, padded)
    flat = ga[:, 0, : HQ * TOPK].reshape(-1)
    place = jnp.stack([ctx // NZ, ctx % NZ]).astype(jnp.int32)
    partial, lse = attend(flat, place, qa, ka, va)
    return project(merge(partial, lse), out_weight)


def solution(mesh):
    return jax.shard_map(
        shards,
        mesh=mesh,
        in_specs=(
            P("ctx", "head"),
            P("ctx", "head"),
            P("ctx", "head"),
            P("ctx", "head", None),
            P("head", None),
        ),
        out_specs=P("ctx", "head"),
        check_vma=False,
    )
```

time: 576 us -> 210 us (0.36)
  waiting for transfers between devices: 270 us -> 43.5 us
  Pallas kernels: 0 us -> 121 us
  loops' own time: 81.9 us -> 0 us
  local copies, waits for them, and re-layouts: 92.7 us -> 14.4 us
  matrix products: 56.5 us -> 0 us
  other arithmetic: 55.2 us -> 5.53 us
  starting transfers between devices: 0.08 us -> 20.6 us
  between operations: 13.2 us -> 0.14 us
    all_gather x2 -> x0, waiting for transfers between devices: 185 us -> none  [the longest x1 98.2 us: shards(): v_piece = lax.all_gather(values, 'ctx', axis=0, tiled=True)]
    pallas_call x0 -> x3, Pallas kernels: none -> 121 us  [the longest x1 51.5 us: gather(): pl.pallas_call(gather_kernel, out_shape=(jax.ShapeDtypeStruct((NY, TOK, H...]
    reduce_scatter x1 -> x0, waiting for transfers between devices: 84.2 us -> none  [shards(): lax.psum_scatter(term.astype(jnp.bfloat16), 'head', scatter_dimension=1,...]
    another operation x129 -> x0, loops' own time: 81.9 us -> none  [the longest x1 81 us: shards(): state = lax.fori_loop(0, piece_blocks, visit, state)]
    dot_general x27 -> x0, matrix products: 56.5 us -> none  [the longest x13 38.3 us: attend_tile(): jnp.dot(expo.astype(jnp.bfloat16), v_tile, preferred_element_type=jnp.flo...]
    squeeze x32 -> x2, local copies, waits for them, and re-layouts: 56.7 us -> 3.51 us  [the longest x1 3.5 us: merge(): got = lax.ppermute(partial[d], 'ctx', pairs)]
    ppermute x0 -> x6, waiting for transfers between devices: none -> 43.5 us  [the longest x3 43.5 us: merge(): got_lse = lax.ppermute(lse[d], 'ctx', pairs)]
    reduce_or x32 -> x0, other arithmetic: 26.4 us -> none  [visit(): jnp.any(gates[qblock, head_pos] == block_pos)]
  transfers between devices with their start and end apart: 3 -> 6, of which waited for: 3 -> 2; matrix products, arithmetic and copies ran while one was open for 2% -> 0% of each run, Pallas kernels for 0% -> 0%
where the time goes in v1:
time: 210 us; the launch traced here: 206 us
  Pallas kernels  121 us (58%)
  waiting for transfers between devices  43.5 us (21%)
  starting transfers between devices  20.6 us (10%)
  local copies, waits for them, and re-layouts  14.4 us (7%)
  other arithmetic  5.53 us (3%)
    pallas_call x1, Pallas kernels, gather(): pl.pallas_call(gather_kernel, out_shape=(jax.ShapeDtypeStruct((NY, TOK, H...  51.5 us
    pallas_call x1, Pallas kernels, project(): pl.pallas_call(project_kernel, out_shape=jax.ShapeDtypeStruct((TOK, width...  44.1 us
    ppermute x3, waiting for transfers between devices, merge(): got_lse = lax.ppermute(lse[d], 'ctx', pairs)  43.5 us
    pallas_call x1, Pallas kernels, attend(): pl.pallas_call(attend_kernel, out_shape=(jax.ShapeDtypeStruct((NY, TOK, H...  25.7 us
    ppermute x3, starting transfers between devices, merge(): got = lax.ppermute(partial[d], 'ctx', pairs)  14.9 us
    ppermute x3, starting transfers between devices, merge(): got_lse = lax.ppermute(lse[d], 'ctx', pairs)  5.74 us
    broadcast_in_dim x4, local copies, waits for them, and re-layouts, merge(): wide = jnp.repeat(w[d].T, HS, axis=1)  4.93 us
    convert_element_type x1, other arithmetic, merge(): return total.astype(BF16)  4.77 us
  transfers between devices with their start and end apart: 6, of which 2 were waited for; matrix products, arithmetic and copies ran while one was open for 0% of the time, Pallas kernels for 0%

profile of v1, /device:TPU:233, one launch (start us, length us, event | category | flops | bytes accessed | tf_op | source)
XLA Modules:
  0.0 205.6 jit_solution(5303299736537464878)
XLA Ops:
  0.0 0.8 copy.11
  0.9 0.6 scatter.4.g_ref
  1.5 51.5 %gather.1 = (bf16[4,1024,512]{2,1,0:T(8,128)(2,1)}, bf16[8,1024,128]{2,1,0:T(8,128)(2,1)}, bf16[8,1024,128]{2,1,0:T(8,128)(2,1)}, s32[4,8,128]{2,1,0:T(8,128)}) custom-call(bf16[1024,512]{1,0:T(8,128)(2,1)} %q_ref.1, bf16[1024,128]{1,0:T(8,128)(2,1)} %k_ref.1, bf16[1024,128]{1,0:T(8,128)(2,1)} %v_ref.1, s32[8,128]{1,0:T(8,128)} %scatter.4.g_ref), custom_call_target="tpu_custom_call" | custom-call | tf_op jit(solution)/shard_map/gather/pallas_call | solution.py:149
  52.9 0.7 slice_reduce_fusion
  53.7 0.6 reshape_squeeze.3.gates
  54.3 0.6 pad_add_fusion.place
  54.9 25.7 %attend.1 = (bf16[4,1024,512]{2,1,0:T(8,128)(2,1)}, f32[4,8,1024]{2,1,0:T(8,128)}) custom-call(s32[48]{0:T(128)} %reshape_squeeze.3.gates, s32[2]{0:T(128)} %pad_add_fusion.place, bf16[4,1024,512]{2,1,0:T(8,128)(2,1)} %get-tuple-element.24.q_ref, bf16[8,1024,128]{2,1,0:T(8,128)(2,1)} %get-tuple-element.25.k_ref, bf16[8,1024,128]{2,1,0:T(8,128)(2,1)} %get-tuple-element.26.v_ref), custom_call_target="tpu_custom_call" | custom-call | tf_op jit(solution)/shard_map/attend/pallas_call | solution.py:263
  80.7 3.5 %slice_bitcast_fusion.2 = (bf16[1024,512]{1,0:T(8,128)(2,1)}, bf16[1024,512]{1,0:T(8,128)(2,1)S(1)}, bf16[1024,512]{1,0:T(8,128)(2,1)}) fusion(bf16[4,1024,512]{2,1,0:T(8,128)(2,1)} %get-tuple-element.28), kind=kLoop, calls=%fused_computation.10 | loop fusion | bytes 6291456 | tf_op jit(solution)/shard_map/squeeze | solution.py:431
  84.2 4.4 %collective-permute-start.3 = (bf16[1024,512]{1,0:T(8,128)(2,1)}, bf16[1024,512]{1,0:T(8,128)(2,1)}, u32[]{:S(2)}, u32[]{:S(2)}) collective-permute-start(bf16[1024,512]{1,0:T(8,128)(2,1)} %get-tuple-element.33), channel_id=1, source_target_pairs={{0,64},{8,72},{16,80},{24,88},{32,96},{40,104},{48,112},{56,120},{... | collective-permute-start | bytes 3145736 | tf_op jit(solution)/shard_map/ppermute | solution.py:431
  88.6 10.5 %collective-permute-start.4 = (bf16[1024,512]{1,0:T(8,128)(2,1)}, bf16[1024,512]{1,0:T(8,128)(2,1)}, u32[]{:S(2)}, u32[]{:S(2)}) collective-permute-start(bf16[1024,512]{1,0:T(8,128)(2,1)} %get-tuple-element.35), channel_id=1, source_target_pairs={{0,128},{8,136},{16,144},{24,152},{32,160},{40,168},{48,176},{56,1... | collective-permute-start | bytes 3145736 | tf_op jit(solution)/shard_map/ppermute | solution.py:431
  99.1 1.5 collective-permute-start
  100.6 1.2 collective-permute-start.1
  101.8 42.5 %collective-permute-done = f32[8,1024]{1,0:T(8,128)S(1)} collective-permute-done((f32[8,1024]{1,0:T(8,128)S(1)}, f32[8,1024]{1,0:T(8,128)S(1)}, u32[]{:S(2)}, u32[]{:S(2)}) %collective-permute-start) | collective-permute-done | bytes 32800 | tf_op jit(solution)/shard_map/ppermute | solution.py:432
  144.4 3.0 %collective-permute-start.2 = (f32[8,1024]{1,0:T(8,128)S(1)}, f32[8,1024]{1,0:T(8,128)S(1)}, u32[]{:S(2)}, u32[]{:S(2)}) collective-permute-start(f32[8,1024]{1,0:T(8,128)S(1)} %get-tuple-element.37), channel_id=1, source_target_pairs={{0,192},{8,200},{16,208},{24,216},{32,224},{40,232},{48,240},{56,2... | collective-permute-start | bytes 98312 | tf_op jit(solution)/shard_map/ppermute | solution.py:432
  147.3 1.0 collective-permute-done.2
  148.7 0.2 copy.13
  149.0 0.2 copy.14
  149.5 1.2 broadcast_in_dim.22
  150.7 1.2 broadcast_in_dim.23
  151.9 1.2 broadcast_in_dim.24
  153.2 1.2 broadcast_in_dim.25
  154.4 4.8 %fusion.1.a_ref = bf16[1024,512]{1,0:T(8,128)(2,1)} fusion(f32[128,8,4,128]{3,2,1,0:T(4,128)S(1)} %bitcast.73, f32[128,8,4,128]{3,2,1,0:T(4,128)S(1)} %bitcast.72, f32[128,8,4,128]{3,2,1,0:T(4,128)S(1)} %bitcast.71, f32[128,8,4,128]{3,2,1,0:T(4,128)S(1)} %bitcast.70, bf16[1024,512]{1,0:T(8,128)(2,1)} %collective-permute-done.5, ...), kind=kLoop, calls=%fused_computation.2 | loop fusion | flops 6291456 | bytes 13631488 | tf_op jit(solution)/shard_map/convert_element_type | solution.py:443
  159.2 44.1 %project.1 = bf16[1024,512]{1,0:T(8,128)(2,1)} custom-call(bf16[1024,512]{1,0:T(8,128)(2,1)} %fusion.1.a_ref, bf16[512,4096]{1,0:T(8,128)(2,1)} %w_ref.1), custom_call_target="tpu_custom_call" | custom-call | tf_op jit(solution)/shard_map/project/pallas_call | solution.py:398
  203.3 2.3 %copy.25 = bf16[1024,512]{1,0:T(8,128)(2,1)} copy(bf16[1024,512]{1,0:T(8,128)(2,1)} %project.1) | data formatting | bytes 2097152
  (15 shorter events, 0.7 us)
Async XLA Ops:
  80.7 18.4 %copy-start = (f32[4,8,1024]{2,1,0:T(8,128)S(1)}, f32[4,8,1024]{2,1,0:T(8,128)}, u32[]{:S(2)}) copy-start(f32[4,8,1024]{2,1,0:T(8,128)} %get-tuple-element.27) | copy-start | bytes 393220
  84.2 65.3 %collective-permute-start.3 = (bf16[1024,512]{1,0:T(8,128)(2,1)}, bf16[1024,512]{1,0:T(8,128)(2,1)}, u32[]{:S(2)}, u32[]{:S(2)}) collective-permute-start(bf16[1024,512]{1,0:T(8,128)(2,1)} %get-tuple-element.33), channel_id=1, source_target_pairs={{0,64},{8,72},{16,80},{24,88},{32,96},{40,104},{48,112},{56,120},{... | collective-permute-start | bytes 3145736 | tf_op jit(solution)/shard_map/ppermute | solution.py:431
  88.6 60.9 %collective-permute-start.4 = (bf16[1024,512]{1,0:T(8,128)(2,1)}, bf16[1024,512]{1,0:T(8,128)(2,1)}, u32[]{:S(2)}, u32[]{:S(2)}) collective-permute-start(bf16[1024,512]{1,0:T(8,128)(2,1)} %get-tuple-element.35), channel_id=1, source_target_pairs={{0,128},{8,136},{16,144},{24,152},{32,160},{40,168},{48,176},{56,1... | collective-permute-start | bytes 3145736 | tf_op jit(solution)/shard_map/ppermute | solution.py:431
  99.1 50.4 %collective-permute-start.5 = (bf16[1024,512]{1,0:T(8,128)(2,1)S(1)}, bf16[1024,512]{1,0:T(8,128)(2,1)}, u32[]{:S(2)}, u32[]{:S(2)}) collective-permute-start(bf16[1024,512]{1,0:T(8,128)(2,1)S(1)} %get-tuple-element.34), channel_id=1, source_target_pairs={{0,192},{8,200},{16,208},{24,216},{32,224},{40,232},{48,240},{56,2... | collective-permute-start | bytes 3145736 | tf_op jit(solution)/shard_map/ppermute | solution.py:431
  99.1 45.3 %collective-permute-start = (f32[8,1024]{1,0:T(8,128)S(1)}, f32[8,1024]{1,0:T(8,128)S(1)}, u32[]{:S(2)}, u32[]{:S(2)}) collective-permute-start(f32[8,1024]{1,0:T(8,128)S(1)} %get-tuple-element.39), channel_id=1, source_target_pairs={{0,64},{8,72},{16,80},{24,88},{32,96},{40,104},{48,112},{56,120},{... | collective-permute-start | bytes 98312 | tf_op jit(solution)/shard_map/ppermute | solution.py:432
  100.6 46.7 %collective-permute-start.1 = (f32[8,1024]{1,0:T(8,128)S(1)}, f32[8,1024]{1,0:T(8,128)S(1)}, u32[]{:S(2)}, u32[]{:S(2)}) collective-permute-start(f32[8,1024]{1,0:T(8,128)S(1)} %get-tuple-element.38), channel_id=1, source_target_pairs={{0,128},{8,136},{16,144},{24,152},{32,160},{40,168},{48,176},{56,1... | collective-permute-start | bytes 98312 | tf_op jit(solution)/shard_map/ppermute | solution.py:432
  144.4 4.0 %collective-permute-start.2 = (f32[8,1024]{1,0:T(8,128)S(1)}, f32[8,1024]{1,0:T(8,128)S(1)}, u32[]{:S(2)}, u32[]{:S(2)}) collective-permute-start(f32[8,1024]{1,0:T(8,128)S(1)} %get-tuple-element.37), channel_id=1, source_target_pairs={{0,192},{8,200},{16,208},{24,216},{32,224},{40,232},{48,240},{56,2... | collective-permute-start | bytes 98312 | tf_op jit(solution)/shard_map/ppermute | solution.py:432

commit v2 on v1

--- a/solution.py
+++ b/solution.py
@@ -292,43 +292,136 @@
 NC = 8
 CR = TOK // NC
 HF = CR // 2
-
-
-def project_kernel(a_ref, w_ref, out_ref, sib_out, sib_in, own, a_out, a_in, b_out, b_in, ss, sr, as_, ar, bs, br):
+LOOK = 2
+WIDTH = HQ * HS
+
+
+def spread(w):
+    t = w.T
+    return jnp.concatenate([jnp.broadcast_to(t[:, h : h + 1], (t.shape[0], HS)) for h in range(HQ)], axis=1)
+
+
+def join(sources):
+    top = functools.reduce(jnp.maximum, [l for l, _ in sources])
+    ws = [jnp.exp2(l - top) for l, _ in sources]
+    total = functools.reduce(jnp.add, ws)
+    inv = 1.0 / total
+    mixed = functools.reduce(jnp.add, [spread(w * inv) * p.astype(F32) for w, (_, p) in zip(ws, sources)])
+    return mixed.astype(BF16), top + jnp.log2(total)
+
+
+def project_kernel(
+    p_ref, l_ref, w_hbm, out_ref,
+    w_ref, p0, p1, r1, r2, r3, m1, l1, l2, l3, lm, att, sib_out, sib_in, own, a_out, a_in, b_out, b_in,
+    loc, ps, pr, ls, lr, ss, sr, as_, ar, bs, br,
+):
     ctx = lax.axis_index("ctx")
     head = lax.axis_index("head")
+    y = ctx // NZ
+    z = ctx % NZ
     x = head // 2
     core = head % 2
     sibling = x * 2 + (1 - core)
     right = ((x + 1) % NX) * 2 + core
     left = ((x + NX - 1) % NX) * 2 + core
     beside = [right, left]
-    width = HQ * HS
+    above = ((y + 1) % NY) * NZ + z
+    below = ((y + NY - 1) % NY) * NZ + z
+
+    local = [
+        pltpu.make_async_copy(p_ref.at[0], p0, loc.at[0]),
+        pltpu.make_async_copy(p_ref.at[1], p1, loc.at[1]),
+        pltpu.make_async_copy(w_hbm, w_ref, loc.at[2]),
+    ]
+    for c in local:
+        c.start()
 
     barrier = pltpu.get_barrier_semaphore()
-    for other in [sibling, right, left]:
-        pl.semaphore_signal(barrier, inc=1, device_id=dev(ctx, other), device_id_type=MESH)
-    pl.semaphore_wait(barrier, 3)
+    for other in [(ctx, sibling), (ctx, right), (ctx, left), (above, head), (below, head)]:
+        pl.semaphore_signal(barrier, inc=1, device_id=other, device_id_type=MESH)
+    pl.semaphore_wait(barrier, 5)
 
     def remote(src, dst, s, r, to):
         return pltpu.make_async_remote_copy(
-            src_ref=src, dst_ref=dst, send_sem=s, recv_sem=r, device_id=dev(ctx, to), device_id_type=MESH
+            src_ref=src, dst_ref=dst, send_sem=s, recv_sem=r, device_id=to, device_id_type=MESH
         )
 
+    def rows_of(r):
+        return pl.ds(pl.multiple_of(r * CR, CR), CR)
+
+    def ret_copies(kind, r, merged=False):
+        at = rows_of(r)
+        dst, ldst = ((r1, l1), (r2, l2), (r3, l3))[kind]
+        if merged:
+            src, lsrc = m1.at[at], lm.at[r]
+        else:
+            src, lsrc = p_ref.at[kind + 1, at], l_ref.at[kind + 1, :, at]
+        to = (below if kind == 2 else above, head)
+        return [
+            remote(src, dst.at[at], ps.at[kind, r], pr.at[kind, r], to),
+            remote(lsrc, ldst.at[r], ls.at[kind, r], lr.at[kind, r], to),
+        ]
+
+    def send_plain(r):
+        @pl.when(y + 2 < NY)
+        def _():
+            for c in ret_copies(1, r):
+                c.start()
+
+        @pl.when(y == 0)
+        def _():
+            for c in ret_copies(0, r) + ret_copies(2, r):
+                c.start()
+
+    def relay(r):
+        @pl.when((y >= 1) & (y + 1 < NY))
+        def _():
+            for c in ret_copies(1, r):
+                c.wait_recv()
+            at = rows_of(r)
+            mixed, lse = join([(l_own(1, r), p1[at, :]), (l2[r], r2[at, :])])
+            m1[at, :] = mixed
+            lm[r] = lse
+            for c in ret_copies(0, r, True):
+                c.start()
+
+    def l_own(slot, r):
+        return l_ref[slot, :, rows_of(r)]
+
+    def home(r):
+        at = rows_of(r)
+
+        @pl.when(y == 0)
+        def _():
+            att[...] = p0[at, :]
+
+        @pl.when((y >= 1) & (y + 1 < NY))
+        def _():
+            for c in ret_copies(0, r):
+                c.wait_recv()
+            att[...] = join([(l_own(0, r), p0[at, :]), (l1[r], r1[at, :])])[0]
+
+        @pl.when(y == NY - 1)
+        def _():
+            for c in ret_copies(0, r) + ret_copies(2, r):
+                c.wait_recv()
+            att[...] = join([(l_own(0, r), p0[at, :]), (l1[r], r1[at, :]), (l3[r], r3[at, :])])[0]
+
     def sib_copy(r):
-        return remote(sib_out.at[r], sib_in.at[r], ss.at[r], sr.at[r], sibling)
+        return remote(sib_out.at[r], sib_in.at[r], ss.at[r], sr.at[r], (ctx, sibling))
 
     def a_copy(r, side):
-        return remote(a_out.at[r, side], a_in.at[r, side], as_.at[r, side], ar.at[r, side], beside[side])
+        return remote(a_out.at[r, side], a_in.at[r, side], as_.at[r, side], ar.at[r, side], (ctx, beside[side]))
 
     def b_copy(r, side):
-        return remote(b_out.at[r, side], b_in.at[r, side], bs.at[r, side], br.at[r, side], beside[side])
+        return remote(b_out.at[r, side], b_in.at[r, side], bs.at[r, side], br.at[r, side], (ctx, beside[side]))
 
     def columns(k, c):
-        return pl.ds(pl.multiple_of((((x + k) % NX) * 2 + c) * width, width), width)
+        return pl.ds(pl.multiple_of((((x + k) % NX) * 2 + c) * WIDTH, WIDTH), WIDTH)
 
     def stage0(r):
-        rows = a_ref[pl.ds(pl.multiple_of(r * CR, CR), CR), :]
+        home(r)
+        rows = att[...]
         for k in range(NX):
             t = jnp.dot(rows, w_ref[:, columns(k, 1 - core)], preferred_element_type=F32)
             sib_out[r, k] = t.astype(BF16)
@@ -359,30 +452,46 @@
         b_copy(r, 0).wait_recv()
         b_copy(r, 1).wait_recv()
         total = pair(r, 0, pl.ds(0, CR)) + b_in[r, 0].astype(F32) + b_in[r, 1].astype(F32)
-        out_ref[pl.ds(pl.multiple_of(r * CR, CR), CR), :] = total.astype(BF16)
+        out_ref[rows_of(r), :] = total.astype(BF16)
+
+    def when(cond, f, r):
+        @pl.when(cond)
+        def _():
+            f(r)
+
+    for r in range(LOOK):
+        send_plain(r)
+    for c in local:
+        c.wait()
+    relay(0)
 
     def step(t, carry):
-        @pl.when(t < NC)
-        def _():
-            stage0(t)
-
-        @pl.when((t >= 1) & (t < NC + 1))
-        def _():
-            stage1(t - 1)
-
-        @pl.when((t >= 2) & (t < NC + 2))
-        def _():
-            stage2(t - 2)
-
-        @pl.when(t >= 3)
-        def _():
-            stage3(t - 3)
-
+        when(t + LOOK < NC, send_plain, t + LOOK)
+        when(t + 1 < NC, relay, t + 1)
+        when(t < NC, stage0, t)
+        when((t >= 1) & (t < NC + 1), stage1, t - 1)
+        when((t >= 2) & (t < NC + 2), stage2, t - 2)
+        when(t >= 3, stage3, t - 3)
         return carry
 
     lax.fori_loop(0, NC + 3, step, 0)
 
     def finish(r, carry):
+        @pl.when(y + 1 < NY)
+        def _():
+            for c in ret_copies(0, r):
+                c.wait_send()
+
+        @pl.when(y + 2 < NY)
+        def _():
+            for c in ret_copies(1, r):
+                c.wait_send()
+
+        @pl.when(y == 0)
+        def _():
+            for c in ret_copies(2, r):
+                c.wait_send()
+
         sib_copy(r).wait_send()
         for side in (0, 1):
             a_copy(r, side).wait_send()
@@ -392,55 +501,37 @@
     lax.fori_loop(0, NC, finish, 0)
 
 
-def project(attention, weight):
-    width = HQ * HS
+def project(partial, lse, weight):
     vmem = pl.BlockSpec(memory_space=pltpu.VMEM)
+    hbm = pl.BlockSpec(memory_space=pl.ANY)
+    sem = pltpu.SemaphoreType.DMA
     return pl.pallas_call(
         project_kernel,
-        out_shape=jax.ShapeDtypeStruct((TOK, width), BF16),
-        in_specs=[vmem] * 2,
+        out_shape=jax.ShapeDtypeStruct((TOK, WIDTH), BF16),
+        in_specs=[hbm, vmem, hbm],
         out_specs=vmem,
         scratch_shapes=[
-            pltpu.VMEM((NC, NX, CR, width), BF16),
-            pltpu.VMEM((NC, NX, CR, width), BF16),
-            pltpu.VMEM((NC, NX, CR, width), BF16),
-            pltpu.VMEM((NC, 2, HF, width), BF16),
-            pltpu.VMEM((NC, 2, HF, width), BF16),
-            pltpu.VMEM((NC, 2, CR, width), BF16),
-            pltpu.VMEM((NC, 2, CR, width), BF16),
-            pltpu.SemaphoreType.DMA((NC,)),
-            pltpu.SemaphoreType.DMA((NC,)),
-            pltpu.SemaphoreType.DMA((NC, 2)),
-            pltpu.SemaphoreType.DMA((NC, 2)),
-            pltpu.SemaphoreType.DMA((NC, 2)),
-            pltpu.SemaphoreType.DMA((NC, 2)),
+            pltpu.VMEM(weight.shape, BF16),
+            *[pltpu.VMEM((TOK, WIDTH), BF16)] * 6,
+            *[pltpu.VMEM((NC, 8, CR), F32)] * 4,
+            pltpu.VMEM((CR, WIDTH), BF16),
+            pltpu.VMEM((NC, NX, CR, WIDTH), BF16),
+            pltpu.VMEM((NC, NX, CR, WIDTH), BF16),
+            pltpu.VMEM((NC, NX, CR, WIDTH), BF16),
+            pltpu.VMEM((NC, 2, HF, WIDTH), BF16),
+            pltpu.VMEM((NC, 2, HF, WIDTH), BF16),
+            pltpu.VMEM((NC, 2, CR, WIDTH), BF16),
+            pltpu.VMEM((NC, 2, CR, WIDTH), BF16),
+            sem((3,)),
+            *[sem((3, NC))] * 4,
+            *[sem((NC,))] * 2,
+            *[sem((NC, 2))] * 4,
         ],
         compiler_params=pltpu.CompilerParams(
             collective_id=1, has_side_effects=True, vmem_limit_bytes=VMEM_LIMIT
         ),
         name="project",
-    )(attention, weight)
-
-
-def merge(partial, lse):
-    y = lax.axis_index("ctx") // NZ
-    outs = [partial[0]]
-    lses = [lse[0, :HQ]]
-    for d in (1, 2, 3):
-        pairs = [((yy * NZ + zz), ((yy + d) % NY) * NZ + zz) for yy in range(NY) for zz in range(NZ)]
-        got = lax.ppermute(partial[d], "ctx", pairs)
-        got_lse = lax.ppermute(lse[d], "ctx", pairs)
-        outs.append(got)
-        lses.append(jnp.where(y >= d, got_lse[:HQ], LOW))
-    lses = jnp.stack(lses, 0)
-    top = jnp.max(lses, axis=0)
-    w = jnp.exp2(lses - top[None])
-    w = w / jnp.sum(w, axis=0)[None]
-    total = 0.0
-    for d in range(NY):
-        wide = jnp.repeat(w[d].T, HS, axis=1)
-        total = total + wide * outs[d].astype(F32)
-    return total.astype(BF16)
+    )(partial, lse, weight)
 
 
 def shards(queries, keys, values, gates, out_weight):
@@ -450,7 +541,7 @@
     flat = ga[:, 0, : HQ * TOPK].reshape(-1)
     place = jnp.stack([ctx // NZ, ctx % NZ]).astype(jnp.int32)
     partial, lse = attend(flat, place, qa, ka, va)
-    return project(merge(partial, lse), out_weight)
+    return project(partial, lse, out_weight)
 
 
 def solution(mesh):

time: 210 us -> 170 us (0.81); the launches traced: 206 us -> 169 us
  waiting for transfers between devices: 43.5 us -> 0 us
  Pallas kernels: 121 us -> 163 us
  starting transfers between devices: 20.6 us -> 0 us
  local copies, waits for them, and re-layouts: 14.4 us -> 5.11 us
  other arithmetic: 5.53 us -> 0.61 us
    ppermute x6 -> x0, waiting for transfers between devices: 43.5 us -> none  [the longest x3 43.5 us: merge(): got_lse = lax.ppermute(lse[d], 'ctx', pairs)]
    pallas_call x1, Pallas kernels: 44.1 us -> 73.8 us  [project(): pl.pallas_call(project_kernel, out_shape=jax.ShapeDtypeStruct((TOK, WIDTH...]
    ppermute x6 -> x0, starting transfers between devices: 20.6 us -> none  [the longest x3 14.9 us: merge(): got = lax.ppermute(partial[d], 'ctx', pairs)]
    pallas_call x1, Pallas kernels: 25.7 us -> 38.2 us  [attend(): pl.pallas_call(attend_kernel, out_shape=(jax.ShapeDtypeStruct((NY, TOK, H...]
    broadcast_in_dim x4 -> x0, local copies, waits for them, and re-layouts: 4.93 us -> none  [merge(): wide = jnp.repeat(w[d].T, HS, axis=1)]
    convert_element_type x1 -> x0, other arithmetic: 4.77 us -> none  [merge(): return total.astype(BF16)]
    squeeze x2 -> x0, local copies, waits for them, and re-layouts: 3.51 us -> none  [the longest x1 3.5 us: merge(): got = lax.ppermute(partial[d], 'ctx', pairs)]
  transfers between devices with their start and end apart: 6 -> 0, of which waited for: 2 -> 0; matrix products, arithmetic and copies ran while one was open for 0% -> 0% of each run, Pallas kernels for 0% -> 0%
where the time goes in v2:
time: 170 us; the launch traced here: 169 us
  Pallas kernels  163 us (96%)
  local copies, waits for them, and re-layouts  5.11 us (3%)
    pallas_call x1, Pallas kernels, project(): pl.pallas_call(project_kernel, out_shape=jax.ShapeDtypeStruct((TOK, WIDTH...  73.8 us
    pallas_call x1, Pallas kernels, gather(): pl.pallas_call(gather_kernel, out_shape=(jax.ShapeDtypeStruct((NY, TOK, H...  51.5 us
    pallas_call x1, Pallas kernels, attend(): pl.pallas_call(attend_kernel, out_shape=(jax.ShapeDtypeStruct((NY, TOK, H...  38.2 us

profile of v2, /device:TPU:233, one launch (start us, length us, event | category | flops | bytes accessed | tf_op | source)
XLA Modules:
  0.0 169.2 jit_solution(15855339246894285285)
XLA Ops:
  0.0 0.6 pad_add_fusion.place
  0.6 0.8 copy.7
  1.4 0.1 reshape.33
  1.5 0.6 scatter.4.g_ref
  2.1 51.5 %gather.1 = (bf16[4,1024,512]{2,1,0:T(8,128)(2,1)}, bf16[8,1024,128]{2,1,0:T(8,128)(2,1)}, bf16[8,1024,128]{2,1,0:T(8,128)(2,1)}, s32[4,8,128]{2,1,0:T(8,128)}) custom-call(bf16[1024,512]{1,0:T(8,128)(2,1)} %q_ref.1, bf16[1024,128]{1,0:T(8,128)(2,1)} %k_ref.1, bf16[1024,128]{1,0:T(8,128)(2,1)} %v_ref.1, s32[8,128]{1,0:T(8,128)} %scatter.4.g_ref), custom_call_target="tpu_custom_call" | custom-call | tf_op jit(solution)/shard_map/gather/pallas_call | solution.py:149
  53.6 0.7 slice_reduce_fusion
  54.3 0.7 reshape_squeeze.3.gates
  55.0 38.2 %attend.1 = (bf16[4,1024,512]{2,1,0:T(8,128)(2,1)}, f32[4,8,1024]{2,1,0:T(8,128)}) custom-call(s32[48]{0:T(128)} %reshape_squeeze.3.gates, s32[2]{0:T(128)} %pad_add_fusion.place, bf16[4,1024,512]{2,1,0:T(8,128)(2,1)} %get-tuple-element.24.q_ref, bf16[8,1024,128]{2,1,0:T(8,128)(2,1)} %get-tuple-element.25.k_ref, bf16[8,1024,128]{2,1,0:T(8,128)(2,1)} %get-tuple-element.26.v_ref), custom_call_target="tpu_custom_call" | custom-call | tf_op jit(solution)/shard_map/attend/pallas_call | solution.py:263
  93.2 73.8 %project.1 = bf16[1024,512]{1,0:T(8,128)(2,1)} custom-call(bf16[4,1024,512]{2,1,0:T(8,128)(2,1)} %get-tuple-element.27.p_ref, f32[4,8,1024]{2,1,0:T(8,128)} %get-tuple-element.28.l_ref, bf16[512,4096]{1,0:T(8,128)(2,1)} %w_hbm.1), custom_call_target="tpu_custom_call" | custom-call | tf_op jit(solution)/shard_map/project/pallas_call | solution.py:508
  167.0 2.3 %copy.9 = bf16[1024,512]{1,0:T(8,128)(2,1)} copy(bf16[1024,512]{1,0:T(8,128)(2,1)} %project.1) | data formatting | bytes 2097152

commit v3 on v2

--- a/solution.py
+++ b/solution.py
@@ -23,11 +23,47 @@
 QCH = 4
 
 
+RT = 256
+NT = TOK // RT
+SAFE = 2.0**100
+WIDTH = HQ * HS
+
+
+def at(i):
+    return pl.ds(i * RT, RT)
+
+
+def wide(m, n):
+    return jnp.concatenate([m] * (n // HS), axis=1)
+
+
+def raw_scores(q, k):
+    return lax.dot_general(q, k, (((1,), (1,)), ((), ())), preferred_element_type=F32)
+
+
+def row_max(s):
+    return jnp.broadcast_to(jnp.max(s, axis=1, keepdims=True) * SCALE2, (s.shape[0], HS))
+
+
+def weights(s, m):
+    return jnp.exp2(s * SCALE2 - wide(m, s.shape[1])).astype(BF16)
+
+
+def as_row(m):
+    eye = lax.broadcasted_iota(jnp.int32, (HS, HS), 0) == lax.broadcasted_iota(jnp.int32, (HS, HS), 1)
+    pieces = [
+        jnp.sum(jnp.where(eye, m[r : r + HS], 0.0), axis=0, keepdims=True) for r in range(0, m.shape[0], HS)
+    ]
+    return jnp.concatenate(pieces, axis=1)
+
+
 def dev(ctx, head):
     return (ctx, head)
 
 
-def gather_kernel(q_ref, k_ref, v_ref, g_ref, qa, ka, va, ga, kv_s, kv_r, q_s, q_r, g_s, g_r, loc):
+def gather_kernel(
+    q_ref, k_ref, v_ref, g_ref, qa, ka, va, ga, oc, lc, vx, ov, lv, kv_s, kv_r, q_s, q_r, g_s, g_r, loc, res
+):
     ctx = lax.axis_index("ctx")
     head = lax.axis_index("head")
     y = ctx // NZ
@@ -93,8 +129,35 @@
     for c in own_copies:
         c.start()
 
+    vx[:, :HS] = v_ref[...]
+    vx[:, HS:] = jnp.ones((TOK, HS), BF16)
+
+    def result_copies(h):
+        return [
+            pltpu.make_async_copy(ov.at[:, pl.ds(h * HS, HS)], oc.at[:, pl.ds(h * HS, HS)], res.at[0, h]),
+            pltpu.make_async_copy(lv.at[h], lc.at[h], res.at[1, h]),
+        ]
+
+    def causal(h):
+        lanes = pl.ds(h * HS, HS)
+        for i in range(NT):
+            n = (i + 1) * RT
+            s = raw_scores(q_ref[at(i), lanes], k_ref[0:n, :])
+            r = lax.broadcasted_iota(jnp.int32, (RT, n), 0) + (n - RT)
+            c = lax.broadcasted_iota(jnp.int32, (RT, n), 1)
+            s = jnp.where(r >= c, s, LOW)
+            m = row_max(s)
+            mixed = jnp.dot(weights(s, m), vx[0:n, :], preferred_element_type=F32)
+            total = mixed[:, HS:]
+            ov[at(i), lanes] = (mixed[:, :HS] * (1.0 / total)).astype(BF16)
+            lv[h, at(i), :] = m + jnp.log2(total)
+        for c in result_copies(h):
+            c.start()
+
     for step in range(4):
         for part in (0, 1):
+            if 2 * step + part < HQ:
+                causal(2 * step + part)
             for direction in (0, 1):
                 if part in parts(direction, step):
                     ring_copy(direction, step, part).wait_recv()
@@ -142,6 +205,9 @@
         c.wait()
     for c in own_copies:
         c.wait()
+    for h in range(HQ):
+        for c in result_copies(h):
+            c.wait()
 
 
 def gather(q, k, v, g):
@@ -153,10 +219,15 @@
             jax.ShapeDtypeStruct((NZ, TOK, HS), BF16),
             jax.ShapeDtypeStruct((NZ, TOK, HS), BF16),
             jax.ShapeDtypeStruct((NY, 8, 128), jnp.int32),
+            jax.ShapeDtypeStruct((TOK, WIDTH), BF16),
+            jax.ShapeDtypeStruct((HQ, TOK, HS), F32),
         ),
-        in_specs=[hbm] * 4,
-        out_specs=(hbm,) * 4,
+        in_specs=[pl.BlockSpec(memory_space=pltpu.VMEM)] * 4,
+        out_specs=(hbm,) * 6,
         scratch_shapes=[
+            pltpu.VMEM((TOK, 2 * HS), BF16),
+            pltpu.VMEM((TOK, WIDTH), BF16),
+            pltpu.VMEM((HQ, TOK, HS), F32),
             pltpu.SemaphoreType.DMA((2, 4, 2)),
             pltpu.SemaphoreType.DMA((2, 4, 2)),
             pltpu.SemaphoreType.DMA((3, QCH)),
@@ -164,6 +235,7 @@
             pltpu.SemaphoreType.DMA((3,)),
             pltpu.SemaphoreType.DMA((3,)),
             pltpu.SemaphoreType.DMA((4,)),
+            pltpu.SemaphoreType.DMA((2, HQ)),
         ],
         compiler_params=pltpu.CompilerParams(
             collective_id=0, has_side_effects=True, vmem_limit_bytes=VMEM_LIMIT
@@ -172,147 +244,196 @@
     )(q, k, v, g)
 
 
-RT = 256
-
-
-def attend_kernel(gates, place, q_ref, k_ref, v_ref, out_ref, lse_ref, peak, acc, todo):
-    slot = pl.program_id(0)
-    head = pl.program_id(1)
+def attend_kernel(
+    gates, place, q_hbm, k_hbm, v_hbm, oc_hbm, lc_hbm, out_hbm, lse_ref,
+    q_ref, k_ref, vx, oc_ref, lc_ref, out_ref, peak, acc, todo, sems, out_sems,
+):
     y = place[0]
     z = place[1]
-    mine = (y + slot) * NZ + z
-
-    def tile(i, k_tile, v_ext, first, diagonal):
-        at = pl.ds(i * RT, RT)
-        s = lax.dot_general(
-            q_ref[0, at, :], k_tile, (((1,), (1,)), ((), ())), preferred_element_type=F32
-        )
-        if diagonal:
-            keys = k_tile.shape[0]
-            r = lax.broadcasted_iota(jnp.int32, (RT, keys), 0) + (keys - RT)
-            c = lax.broadcasted_iota(jnp.int32, (RT, keys), 1)
-            s = jnp.where(r >= c, s, LOW)
-        top = jnp.max(s, axis=1, keepdims=True) * SCALE2
-        if first:
-            new = jnp.broadcast_to(top, (RT, HS))
-        else:
-            old = peak[at, :]
-            new = jnp.maximum(old, top)
-        p = jnp.exp2(s * SCALE2 - new[:, :1]).astype(BF16)
-        part = jnp.dot(p, v_ext, preferred_element_type=F32)
-        if first:
-            acc[at, :] = part
-        else:
-            fade = jnp.exp2(old - new)
-            acc[at, :] = acc[at, :] * jnp.concatenate([fade, fade], axis=1) + part
-        peak[at, :] = new
-
-    def extended(block, n):
-        v = v_ref[block, 0:n, :]
-        return jnp.concatenate([v, jnp.ones_like(v)], axis=1)
-
-    count = jnp.int32(0)
-    for j in range(TOPK):
-        g = gates[slot * (HQ * TOPK) + head * TOPK + j]
-        good = (g >= y * NZ) & (g < (y + 1) * NZ) & (g < mine) & (y + slot < NY)
-
-        @pl.when(good)
-        def _(g=g, count=count):
-            todo[count] = g - y * NZ
-
-        count = count + good.astype(jnp.int32)
-
-    @pl.when(slot == 0)
-    def _():
-        for i in range(TOK // RT):
-            n = (i + 1) * RT
-            tile(i, k_ref[z, 0:n, :], extended(z, n), True, True)
-
-    @pl.when((slot > 0) & (count > 0))
-    def _():
-        block = todo[0]
-        for i in range(TOK // RT):
-            tile(i, k_ref[block], extended(block, TOK), True, False)
-
-    def more(e, carry):
-        block = todo[e]
-        for i in range(TOK // RT):
-            tile(i, k_ref[block], extended(block, TOK), False, False)
+
+    shared = [
+        pltpu.make_async_copy(k_hbm, k_ref, sems.at[0]),
+        pltpu.make_async_copy(v_hbm, vx.at[:, :, pl.ds(0, HS)], sems.at[1]),
+        pltpu.make_async_copy(oc_hbm, oc_ref, sems.at[2]),
+        pltpu.make_async_copy(lc_hbm, lc_ref, sems.at[3]),
+    ]
+
+    def query_copy(slot):
+        return pltpu.make_async_copy(q_hbm.at[slot], q_ref.at[slot], sems.at[4 + slot])
+
+    def out_copy(slot):
+        return pltpu.make_async_copy(out_ref.at[slot], out_hbm.at[slot], out_sems.at[slot])
+
+    query_copy(0).start()
+    for c in shared:
+        c.start()
+    for slot in range(1, NY):
+        query_copy(slot).start()
+
+    lse_ref[...] = jnp.full(lse_ref.shape, LOW, F32)
+
+    def fill(block, carry):
+        vx[block, :, HS:] = jnp.ones((TOK, HS), BF16)
         return carry
 
-    lax.fori_loop(jnp.where(slot == 0, 0, 1), count, more, 0)
-
-    some = (slot == 0) | (count > 0)
-
-    @pl.when(some)
-    def _():
-        for i in range(TOK // RT):
-            at = pl.ds(i * RT, RT)
-            total = acc[at, HS:]
-            out_ref[0, at, :] = (acc[at, :HS] / total).astype(BF16)
-            lse = peak[at, :] + jnp.log2(total)
-            lse_ref[0, pl.ds(head, 1), at] = lse.T[0:1, :]
-
-    @pl.when(jnp.logical_not(some))
-    def _():
-        out_ref[...] = jnp.zeros_like(out_ref)
-        lse_ref[0, pl.ds(head, 1), :] = jnp.full((1, TOK), LOW, F32)
-
-
-def attend(gates, place, qa, ka, va):
+    lax.fori_loop(0, NZ, fill, 0)
+    for c in shared:
+        c.wait()
+
+    def one(index, carry):
+        slot = index // HQ
+        head = index % HQ
+        mine = (y + slot) * NZ + z
+        lanes = pl.ds(pl.multiple_of(head * HS, HS), HS)
+
+        @pl.when(head == 0)
+        def _():
+            query_copy(slot).wait()
+
+        def scores(i, block):
+            return raw_scores(q_ref[slot, at(i), lanes], k_ref[block])
+
+        def mix(s, m, block):
+            return jnp.dot(weights(s, m), vx[block], preferred_element_type=F32)
+
+        count = jnp.int32(0)
+        for j in range(TOPK):
+            g = gates[slot * (HQ * TOPK) + head * TOPK + j]
+            good = (g >= y * NZ) & (g < (y + 1) * NZ) & (g < mine) & (y + slot < NY)
+
+            @pl.when(good)
+            def _(g=g, count=count):
+                todo[count] = g - y * NZ
+
+            count = count + good.astype(jnp.int32)
+
+        def start():
+            @pl.when(slot == 0)
+            def _():
+                peak[...] = lc_ref[head]
+                acc[:, :HS] = oc_ref[:, lanes].astype(F32)
+                acc[:, HS:] = jnp.ones((TOK, HS), F32)
+
+        def more(e, carry):
+            block = todo[e]
+            for i in range(NT):
+                acc[at(i), :] += mix(scores(i, block), peak[at(i), :], block)
+            return carry
+
+        def general(e, carry):
+            block = todo[e]
+            for i in range(NT):
+                s = scores(i, block)
+                old = peak[at(i), :]
+                new = jnp.maximum(old, row_max(s))
+                peak[at(i), :] = new
+                acc[at(i), :] = acc[at(i), :] * wide(jnp.exp2(old - new), 2 * HS) + mix(s, new, block)
+            return carry
+
+        @pl.when(count > 0)
+        def _():
+            start()
+
+            @pl.when(slot > 0)
+            def _():
+                block = todo[0]
+                for i in range(NT):
+                    s = scores(i, block)
+                    m = row_max(s[:, :RT])
+                    peak[at(i), :] = m
+                    acc[at(i), :] = mix(s, m, block)
+
+            lax.fori_loop(jnp.where(slot == 0, 0, 1), count, more, 0)
+            fine = jnp.min((acc[:, HS:] < SAFE).astype(F32)) > 0.5
+
+            @pl.when(jnp.logical_not(fine))
+            def _():
+                peak[...] = jnp.full(peak.shape, LOW, F32)
+                acc[...] = jnp.zeros_like(acc)
+                start()
+                lax.fori_loop(0, count, general, 0)
+
+            for i in range(NT):
+                total = acc[at(i), HS:]
+                out_ref[slot, at(i), lanes] = (acc[at(i), :HS] * (1.0 / total)).astype(BF16)
+                lse_ref[slot, pl.ds(head, 1), at(i)] = as_row(peak[at(i), :] + jnp.log2(total))
+
+        @pl.when((count == 0) & (slot == 0))
+        def _():
+            out_ref[slot, :, lanes] = oc_ref[:, lanes]
+            for i in range(NT):
+                lse_ref[slot, pl.ds(head, 1), at(i)] = as_row(lc_ref[head, at(i), :])
+
+        @pl.when((count == 0) & (slot > 0))
+        def _():
+            out_ref[slot, :, lanes] = jnp.zeros((TOK, HS), BF16)
+
+        @pl.when(head == HQ - 1)
+        def _():
+            out_copy(slot).start()
+
+        return carry
+
+    lax.fori_loop(0, NY * HQ, one, 0)
+    for slot in range(NY):
+        out_copy(slot).wait()
+
+
+def attend(gates, place, qa, ka, va, oc, lc):
+    hbm = pl.BlockSpec(memory_space=pl.ANY)
+    smem = pl.BlockSpec(memory_space=pltpu.SMEM)
     return pl.pallas_call(
         attend_kernel,
         out_shape=(
-            jax.ShapeDtypeStruct((NY, TOK, HQ * HS), BF16),
+            jax.ShapeDtypeStruct((NY, TOK, WIDTH), BF16),
             jax.ShapeDtypeStruct((NY, 8, TOK), F32),
         ),
-        grid_spec=pltpu.PrefetchScalarGridSpec(
-            num_scalar_prefetch=2,
-            grid=(NY, HQ),
-            in_specs=[
-                pl.BlockSpec((1, TOK, HS), lambda s, h, *_: (s, 0, h)),
-                pl.BlockSpec((NZ, TOK, HS), lambda s, h, *_: (0, 0, 0)),
-                pl.BlockSpec((NZ, TOK, HS), lambda s, h, *_: (0, 0, 0)),
-            ],
-            out_specs=(
-                pl.BlockSpec((1, TOK, HS), lambda s, h, *_: (s, 0, h)),
-                pl.BlockSpec((1, 8, TOK), lambda s, h, *_: (s, 0, 0)),
-            ),
-            scratch_shapes=[
-                pltpu.VMEM((TOK, HS), F32),
-                pltpu.VMEM((TOK, 2 * HS), F32),
-                pltpu.SMEM((TOPK + 1,), jnp.int32),
-            ],
-        ),
+        in_specs=[smem, smem] + [hbm] * 5,
+        out_specs=(hbm, pl.BlockSpec(memory_space=pltpu.VMEM)),
+        scratch_shapes=[
+            pltpu.VMEM((NY, TOK, WIDTH), BF16),
+            pltpu.VMEM((NZ, TOK, HS), BF16),
+            pltpu.VMEM((NZ, TOK, 2 * HS), BF16),
+            pltpu.VMEM((TOK, WIDTH), BF16),
+            pltpu.VMEM((HQ, TOK, HS), F32),
+            pltpu.VMEM((NY, TOK, WIDTH), BF16),
+            pltpu.VMEM((TOK, HS), F32),
+            pltpu.VMEM((TOK, 2 * HS), F32),
+            pltpu.SMEM((TOPK + 1,), jnp.int32),
+            pltpu.SemaphoreType.DMA((4 + NY,)),
+            pltpu.SemaphoreType.DMA((NY,)),
+        ],
         compiler_params=pltpu.CompilerParams(vmem_limit_bytes=VMEM_LIMIT),
         name="attend",
-    )(gates, place, qa, ka, va)
+    )(gates, place, qa, ka, va, oc, lc)
 
 
 NC = 8
 CR = TOK // NC
 HF = CR // 2
-LOOK = 2
-WIDTH = HQ * HS
-
-
-def spread(w):
-    t = w.T
-    return jnp.concatenate([jnp.broadcast_to(t[:, h : h + 1], (t.shape[0], HS)) for h in range(HQ)], axis=1)
-
-
-def join(sources):
+LOOK = 3
+HALF = WIDTH // 2
+LEFT_HALF = slice(0, HALF)
+RIGHT_HALF = slice(HALF, WIDTH)
+
+
+def join(sources, heads):
     top = functools.reduce(jnp.maximum, [l for l, _ in sources])
     ws = [jnp.exp2(l - top) for l, _ in sources]
     total = functools.reduce(jnp.add, ws)
     inv = 1.0 / total
-    mixed = functools.reduce(jnp.add, [spread(w * inv) * p.astype(F32) for w, (_, p) in zip(ws, sources)])
+    mixed = 0.0
+    for w, (_, p) in zip(ws, sources):
+        t = (w * inv).T
+        wide_w = jnp.concatenate([jnp.broadcast_to(t[:, h : h + 1], (t.shape[0], HS)) for h in heads], axis=1)
+        mixed = mixed + wide_w * p.astype(F32)
     return mixed.astype(BF16), top + jnp.log2(total)
 
 
 def project_kernel(
     p_ref, l_ref, w_hbm, out_ref,
-    w_ref, p0, p1, r1, r2, r3, m1, l1, l2, l3, lm, att, sib_out, sib_in, own, a_out, a_in, b_out, b_in,
+    w_ref, p0, p1, p3, r1, r2, r3, r4, r5, m1, m3, l1, l2, l3, l4, l5, lm1, lm3, att,
+    sib_out, sib_in, own, a_out, a_in, b_out, b_in,
     loc, ps, pr, ls, lr, ss, sr, as_, ar, bs, br,
 ):
     ctx = lax.axis_index("ctx")
@@ -331,7 +452,8 @@
     local = [
         pltpu.make_async_copy(p_ref.at[0], p0, loc.at[0]),
         pltpu.make_async_copy(p_ref.at[1], p1, loc.at[1]),
-        pltpu.make_async_copy(w_hbm, w_ref, loc.at[2]),
+        pltpu.make_async_copy(p_ref.at[3], p3, loc.at[2]),
+        pltpu.make_async_copy(w_hbm, w_ref, loc.at[3]),
     ]
     for c in local:
         c.start()
@@ -349,45 +471,78 @@
     def rows_of(r):
         return pl.ds(pl.multiple_of(r * CR, CR), CR)
 
-    def ret_copies(kind, r, merged=False):
+    def stream(kind, r, merged=False):
         at = rows_of(r)
-        dst, ldst = ((r1, l1), (r2, l2), (r3, l3))[kind]
-        if merged:
-            src, lsrc = m1.at[at], lm.at[r]
+        first, second = pl.ds(0, HALF), pl.ds(HALF, HALF)
+        own_lse = l_ref.at[min(kind, 2) + 1 if kind != 2 else 2, :, at]
+        if kind == 0:
+            src, lsrc = (m1.at[at], lm1.at[r]) if merged else (p_ref.at[1, at], own_lse)
+            dst, ldst = r1.at[at], l1.at[r]
+        elif kind == 1:
+            src, lsrc, dst, ldst = p_ref.at[2, at, first], own_lse, r2.at[at], l2.at[r]
+        elif kind == 2:
+            src, lsrc, dst, ldst = p_ref.at[2, at, second], own_lse, r4.at[at], l4.at[r]
+        elif kind == 3:
+            src, lsrc, dst, ldst = m3.at[at], lm3.at[r], r3.at[at], l3.at[r]
         else:
-            src, lsrc = p_ref.at[kind + 1, at], l_ref.at[kind + 1, :, at]
-        to = (below if kind == 2 else above, head)
+            src, lsrc, dst, ldst = r4.at[at], l4.at[r], r5.at[at], l5.at[r]
+        to = (above if kind < 2 else below, head)
         return [
-            remote(src, dst.at[at], ps.at[kind, r], pr.at[kind, r], to),
-            remote(lsrc, ldst.at[r], ls.at[kind, r], lr.at[kind, r], to),
+            remote(src, dst, ps.at[kind, r], pr.at[kind, r], to),
+            remote(lsrc, ldst, ls.at[kind, r], lr.at[kind, r], to),
         ]
 
-    def send_plain(r):
-        @pl.when(y + 2 < NY)
-        def _():
-            for c in ret_copies(1, r):
-                c.start()
-
-        @pl.when(y == 0)
-        def _():
-            for c in ret_copies(0, r) + ret_copies(2, r):
-                c.start()
-
-    def relay(r):
-        @pl.when((y >= 1) & (y + 1 < NY))
-        def _():
-            for c in ret_copies(1, r):
-                c.wait_recv()
-            at = rows_of(r)
-            mixed, lse = join([(l_own(1, r), p1[at, :]), (l2[r], r2[at, :])])
-            m1[at, :] = mixed
-            lm[r] = lse
-            for c in ret_copies(0, r, True):
-                c.start()
+    def begin(copies):
+        for c in copies:
+            c.start()
+
+    def arrived(copies):
+        for c in copies:
+            c.wait_recv()
 
     def l_own(slot, r):
         return l_ref[slot, :, rows_of(r)]
 
+    def pick(low, high):
+        rows = lax.broadcasted_iota(jnp.int32, low.shape, 0)
+        return jnp.where(rows < HQ // 2, low, high)
+
+    def send_plain(r):
+        @pl.when(y < 2)
+        def _():
+            begin(stream(2, r))
+            begin(stream(1, r))
+
+        @pl.when(y == 0)
+        def _():
+            begin(stream(0, r))
+
+    def relay(r):
+        at = rows_of(r)
+
+        @pl.when((y == 1) | (y == 2))
+        def _():
+            arrived(stream(1, r))
+            mixed, lse = join([(l_own(1, r), p1[at, LEFT_HALF]), (l2[r], r2[at, :])], (0, 1))
+            m1[at, LEFT_HALF] = mixed
+            m1[at, RIGHT_HALF] = p1[at, RIGHT_HALF]
+            lm1[r] = pick(lse, l_own(1, r))
+            begin(stream(0, r, True))
+
+        @pl.when(y == 0)
+        def _():
+            arrived(stream(2, r))
+            mixed, lse = join([(l_own(3, r), p3[at, RIGHT_HALF]), (l4[r], r4[at, :])], (2, 3))
+            m3[at, RIGHT_HALF] = mixed
+            m3[at, LEFT_HALF] = p3[at, LEFT_HALF]
+            lm3[r] = pick(l_own(3, r), lse)
+            begin(stream(3, r))
+
+        @pl.when(y == 3)
+        def _():
+            arrived(stream(2, r))
+            begin(stream(4, r))
+
     def home(r):
         at = rows_of(r)
 
@@ -395,17 +550,24 @@
         def _():
             att[...] = p0[at, :]
 
-        @pl.when((y >= 1) & (y + 1 < NY))
-        def _():
-            for c in ret_copies(0, r):
-                c.wait_recv()
-            att[...] = join([(l_own(0, r), p0[at, :]), (l1[r], r1[at, :])])[0]
-
-        @pl.when(y == NY - 1)
-        def _():
-            for c in ret_copies(0, r) + ret_copies(2, r):
-                c.wait_recv()
-            att[...] = join([(l_own(0, r), p0[at, :]), (l1[r], r1[at, :]), (l3[r], r3[at, :])])[0]
+        @pl.when(y == 1)
+        def _():
+            arrived(stream(0, r))
+            att[...] = join([(l_own(0, r), p0[at, :]), (l1[r], r1[at, :])], range(HQ))[0]
+
+        @pl.when(y == 2)
+        def _():
+            arrived(stream(0, r) + stream(4, r))
+            own_lse = l_own(0, r)
+            att[:, LEFT_HALF] = join([(own_lse, p0[at, LEFT_HALF]), (l1[r], r1[at, LEFT_HALF])], (0, 1))[0]
+            att[:, RIGHT_HALF] = join(
+                [(own_lse, p0[at, RIGHT_HALF]), (l1[r], r1[at, RIGHT_HALF]), (l5[r], r5[at, :])], (2, 3)
+            )[0]
+
+        @pl.when(y == 3)
+        def _():
+            arrived(stream(0, r) + stream(3, r))
+            att[...] = join([(l_own(0, r), p0[at, :]), (l1[r], r1[at, :]), (l3[r], r3[at, :])], range(HQ))[0]
 
     def sib_copy(r):
         return remote(sib_out.at[r], sib_in.at[r], ss.at[r], sr.at[r], (ctx, sibling))
@@ -476,21 +638,26 @@
 
     lax.fori_loop(0, NC + 3, step, 0)
 
+    def sent(copies):
+        for c in copies:
+            c.wait_send()
+
     def finish(r, carry):
-        @pl.when(y + 1 < NY)
-        def _():
-            for c in ret_copies(0, r):
-                c.wait_send()
-
-        @pl.when(y + 2 < NY)
-        def _():
-            for c in ret_copies(1, r):
-                c.wait_send()
+        @pl.when(y < 3)
+        def _():
+            sent(stream(0, r))
+
+        @pl.when(y < 2)
+        def _():
+            sent(stream(1, r) + stream(2, r))
 
         @pl.when(y == 0)
         def _():
-            for c in ret_copies(2, r):
-                c.wait_send()
+            sent(stream(3, r))
+
+        @pl.when(y == 3)
+        def _():
+            sent(stream(4, r))
 
         sib_copy(r).wait_send()
         for side in (0, 1):
@@ -505,6 +672,8 @@
     vmem = pl.BlockSpec(memory_space=pltpu.VMEM)
     hbm = pl.BlockSpec(memory_space=pl.ANY)
     sem = pltpu.SemaphoreType.DMA
+    full = pltpu.VMEM((TOK, WIDTH), BF16)
+    half = pltpu.VMEM((TOK, HALF), BF16)
     return pl.pallas_call(
         project_kernel,
         out_shape=jax.ShapeDtypeStruct((TOK, WIDTH), BF16),
@@ -512,8 +681,10 @@
         out_specs=vmem,
         scratch_shapes=[
             pltpu.VMEM(weight.shape, BF16),
-            *[pltpu.VMEM((TOK, WIDTH), BF16)] * 6,
-            *[pltpu.VMEM((NC, 8, CR), F32)] * 4,
+            full, full, full,
+            full, half, full, half, half,
+            full, full,
+            *[pltpu.VMEM((NC, 8, CR), F32)] * 7,
             pltpu.VMEM((CR, WIDTH), BF16),
             pltpu.VMEM((NC, NX, CR, WIDTH), BF16),
             pltpu.VMEM((NC, NX, CR, WIDTH), BF16),
@@ -522,8 +693,8 @@
             pltpu.VMEM((NC, 2, HF, WIDTH), BF16),
             pltpu.VMEM((NC, 2, CR, WIDTH), BF16),
             pltpu.VMEM((NC, 2, CR, WIDTH), BF16),
-            sem((3,)),
-            *[sem((3, NC))] * 4,
+            sem((4,)),
+            *[sem((5, NC))] * 4,
             *[sem((NC,))] * 2,
             *[sem((NC, 2))] * 4,
         ],
@@ -537,10 +708,10 @@
 def shards(queries, keys, values, gates, out_weight):
     ctx = lax.axis_index("ctx")
     padded = jnp.zeros((8, 128), jnp.int32).at[0, : HQ * TOPK].set(gates.reshape(-1))
-    qa, ka, va, ga = gather(queries, keys, values, padded)
+    qa, ka, va, ga, oc, lc = gather(queries, keys, values, padded)
     flat = ga[:, 0, : HQ * TOPK].reshape(-1)
     place = jnp.stack([ctx // NZ, ctx % NZ]).astype(jnp.int32)
-    partial, lse = attend(flat, place, qa, ka, va)
+    partial, lse = attend(flat, place, qa, ka, va, oc, lc)
     return project(partial, lse, out_weight)
 
 

time: 170 us -> 153 us (0.900)
  the two profiles are of different devices: /device:TPU:233 before, /device:TPU:176 now
where the time goes in v3:
time: 153 us
  Pallas kernels  147 us (96%)
  local copies, waits for them, and re-layouts  5.11 us (3%)
    pallas_call x1, Pallas kernels, project(): pl.pallas_call(project_kernel, out_shape=jax.ShapeDtypeStruct((TOK, WIDTH...  84.5 us
    pallas_call x1, Pallas kernels, gather(): pl.pallas_call(gather_kernel, out_shape=(jax.ShapeDtypeStruct((NY, TOK, H...  49.5 us
    pallas_call x1, Pallas kernels, attend(): pl.pallas_call(attend_kernel, out_shape=(jax.ShapeDtypeStruct((NY, TOK, W...  13 us

profile of v3, /device:TPU:176, one launch (start us, length us, event | category | flops | bytes accessed | tf_op | source)
XLA Modules:
  0.0 152.7 jit_solution(8506170956369197832)
XLA Ops:
  0.0 0.6 pad_add_fusion.place
  0.6 0.8 copy.7
  1.4 0.1 reshape.33
  1.5 0.6 scatter.4.g_ref
  2.1 49.5 %gather.1 = (bf16[4,1024,512]{2,1,0:T(8,128)(2,1)}, bf16[8,1024,128]{2,1,0:T(8,128)(2,1)}, bf16[8,1024,128]{2,1,0:T(8,128)(2,1)}, s32[4,8,128]{2,1,0:T(8,128)}, ...) custom-call(bf16[1024,512]{1,0:T(8,128)(2,1)} %q_ref.1, bf16[1024,128]{1,0:T(8,128)(2,1)} %k_ref.1, ...), custom_call_target="tpu_custom_call" | custom-call | tf_op jit(solution)/shard_map/gather/pallas_call | solution.py:215
  51.6 0.7 slice_reduce_fusion
  52.3 0.7 reshape_squeeze.3.gates
  53.0 13.0 %attend.1 = (bf16[4,1024,512]{2,1,0:T(8,128)(2,1)}, f32[4,8,1024]{2,1,0:T(8,128)}) custom-call(s32[48]{0:T(128)} %reshape_squeeze.3.gates, s32[2]{0:T(128)} %pad_add_fusion.place, bf16[4,1024,512]{2,1,0:T(8,128)(2,1)} %get-tuple-element.26.q_hbm, bf16[8,1024,128]{2,1,0:T(8,128)(2,1)} %get-tuple-element.27.k_hbm, ...), custom_call_target="tpu_custom_call" | custom-call | tf_op jit(solution)/shard_map/attend/pallas_call | solution.py:385
  65.9 84.5 %project.1 = bf16[1024,512]{1,0:T(8,128)(2,1)} custom-call(bf16[4,1024,512]{2,1,0:T(8,128)(2,1)} %get-tuple-element.31.p_ref, f32[4,8,1024]{2,1,0:T(8,128)} %get-tuple-element.32.l_ref, bf16[512,4096]{1,0:T(8,128)(2,1)} %w_hbm.1), custom_call_target="tpu_custom_call" | custom-call | tf_op jit(solution)/shard_map/project/pallas_call | solution.py:677
  150.4 2.3 %copy.9 = bf16[1024,512]{1,0:T(8,128)(2,1)} copy(bf16[1024,512]{1,0:T(8,128)(2,1)} %project.1) | data formatting | bytes 2097152
